TPU v7x, 256 devices: a whole 4x4x8 slice. The times are simulated.
256 devices in a mesh: dp: 8 (over z), fsdp: 32 (over x, y, core).
Axes of the slice: x: 4, y: 4, z: 8, core: 2. Of those that a mesh axis runs over, the one named last changes fastest.
Arguments:
- replica_grads: bfloat16 [8, 2, 7168, 768], P('dp', None, 'fsdp'), may hold values from -600 to 600
- momentum: float32 [2, 7168, 768], P(None, 'fsdp'), may hold values from -18 to 18
- weights: float32 [2, 7168, 768], P(None, 'fsdp'), may hold values from -6 to 6
Outputs:
- new_momentum: float32 [2, 7168, 768], P(None, 'fsdp')
- update: float32 [2, 7168, 768], P(None, 'fsdp')
- new_weights: float32 [2, 7168, 768], P(None, 'fsdp')
All inputs are finite; a program needn't handle non-finite values.
Results may differ from a plain program's by a relative error of at most 0.0003.
Values sent between devices are 32-bit elements; how exact they have to be, the bound alone decides.
A program may use at most 64 MiB of HBM per device.

v0:
```python
import math

import jax
import jax.numpy as jnp
from jax import lax
from jax.sharding import PartitionSpec as P

D = 7168
R = 768
ITERS = 2


QUINTIC_LINEAR = 3.4445
QUINTIC_CUBIC = -4.775
QUINTIC_FIFTH = 2.0315
MOMENTUM_FACTOR = 0.95
LEARNING_RATE = 0.02
WEIGHT_DECAY = 0.1
NORM_EPSILON = 1e-07
UPDATE_FACTOR = 0.2


def full_gram(operand, factor, reduce_terms, spread_rows):

    def partial_gram(first_row, row_count):
        return jnp.einsum(
            "ogn,ogs->nos",
            operand,
            operand,
            preferred_element_type=jnp.float32,
            precision=lax.Precision.HIGHEST,
        )

    shares = reduce_terms(partial_gram)
    if factor is not None:
        shares = shares * factor[None, :, None]
    return spread_rows(shares)


def newton_schulz(stacks, inverse, gram_builder):
    current = stacks
    for iteration in range(ITERS):
        factor = inverse * inverse if iteration == 0 else None
        gram_whole = gram_builder(current, factor)
        product = jnp.einsum(
            "lir,rlc->lic",
            current,
            gram_whole,
            preferred_element_type=jnp.float32,
            precision=lax.Precision.HIGHEST,
        )
        second = jnp.einsum(
            "lir,rlc->lic",
            product,
            gram_whole,
            preferred_element_type=jnp.float32,
            precision=lax.Precision.HIGHEST,
        )
        current = QUINTIC_LINEAR * current + QUINTIC_CUBIC * product + QUINTIC_FIFTH * second
        if iteration == 0:
            current = current * inverse[:, None, None]
    return current


def shards(replica_grads, momentum, weights):
    local_grads = replica_grads[0].astype(jnp.float32)
    layer_count = momentum.shape[0]
    total_width = momentum.shape[2]
    summed = lax.psum(local_grads, "dp")

    def reduce_terms(partial_fn):
        return lax.psum_scatter(
            partial_fn(jnp.int32(0), total_width // lax.axis_size("fsdp") * lax.axis_size("fsdp")),
            "fsdp",
            scatter_dimension=0,
            tiled=True,
        )

    def spread_rows(shares):
        return lax.all_gather(shares, "fsdp", axis=0, tiled=True)

    def gram_builder(operand, factor):
        return full_gram(operand, factor, reduce_terms, spread_rows)

    new_momentum = MOMENTUM_FACTOR * momentum + summed
    direction = summed + MOMENTUM_FACTOR * new_momentum
    squares_sum = lax.psum(jnp.sum(direction * direction, axis=(1, 2)), "fsdp")
    inverse = 1.0 / (jnp.sqrt(squares_sum) + NORM_EPSILON)
    orthogonal = jnp.concatenate(
        [
            newton_schulz(
                direction[layer_index : layer_index + 1],
                inverse[layer_index : layer_index + 1],
                gram_builder,
            )
            for layer_index in range(layer_count)
        ],
        axis=0,
    )
    update = UPDATE_FACTOR * math.sqrt(max(D, R)) * orthogonal
    new_weights = weights - LEARNING_RATE * (update + WEIGHT_DECAY * weights)
    return (new_momentum, update, new_weights)


def solution(mesh):
    return jax.shard_map(
        shards,
        mesh=mesh,
        in_specs=(P("dp", None, "fsdp", None), P(None, "fsdp", None), P(None, "fsdp", None)),
        out_specs=(P(None, "fsdp", None), P(None, "fsdp", None), P(None, "fsdp", None)),
        check_vma=False,
    )
```

profile of v0, /device:TPU:1, one launch (start us, length us, event | category | flops | bytes accessed | tf_op | source)
XLA Modules:
  0.0 599.9 jit_solution(377930329086340686)
XLA Ops:
  7.2 2.4 bitcast_convert_fusion
  9.7 79.0 %all-reduce.10.cloned.1.call-done = f32[2,224,768]{2,1,0:T(8,128)} async-done(((f32[2,224,768]{2,1,0:T(8,128)}), f32[2,224,768]{2,1,0:T(8,128)}) %all-reduce.10.cloned.1.call-update) | async-done | bytes 1376272 | tf_op jit(solution)/shard_map/psum | solution.py:69
  88.7 2.7 multiply_reduce_fusion
  91.4 3.5 convolution_bitcast_fusion.3
  94.9 3.5 convolution_bitcast_fusion.1
  98.4 6.7 %copy.6 = f32[768,1,768]{2,1,0:T(1,128)} copy(f32[768,1,768]{0,2,1:T(8,128)} %convolution_bitcast_fusion.3) | data formatting | bytes 4718592 | tf_op jit(solution)/shard_map/ogn,ogs->nos/transpose | solution.py:26
  105.1 6.7 %copy.8 = f32[768,1,768]{2,1,0:T(1,128)} copy(f32[768,1,768]{0,2,1:T(8,128)} %convolution_bitcast_fusion.1) | data formatting | bytes 4718592 | tf_op jit(solution)/shard_map/ogn,ogs->nos/transpose | solution.py:26
  113.7 66.7 %psum.15 = f32[2]{0:T(128)S(1)} all-reduce(f32[2]{0:T(128)S(1)} %get-tuple-element.9), channel_id=1, replica_groups=mesh['dp'=8,'fsdp'=32] {'fsdp'}, use_global_device_ids=true, to_apply=%region_3.0 | all-reduce | flops 2 | bytes 16 | tf_op jit(solution)/shard_map/psum | solution.py:87
  182.2 55.4 %all-reduce.14.cloned.1.call-done = (f32[768,1,768]{2,1,0:T(1,128)}, f32[768,1,768]{2,1,0:T(1,128)}) async-done(((f32[768,1,768]{2,1,0:T(1,128)}, f32[768,1,768]{2,1,0:T(1,128)}), (f32[768,1,768]{2,1,0:T(1,128)}, f32[768,1,768]{2,1,0:T(1,128)})) %all-reduce.14.cloned.1.call-update) | async-done | bytes 4718608
  242.1 48.1 %all-gather.5.cloned.1.call-done = f32[768,1,768]{2,1,0:T(1,128)} async-done(((f32[24,1,768]{2,1,0:T(1,128)}), f32[768,1,768]{2,1,0:T(1,128)}) %all-gather.5.cloned.1.call-update) | async-done | bytes 2359312 | tf_op jit(solution)/shard_map/all_gather | solution.py:80
  290.2 3.8 fusion.14
  294.0 2.7 fusion.63
  296.6 3.5 convolution_bitcast_fusion.2
  300.2 6.7 %copy.7 = f32[768,1,768]{2,1,0:T(1,128)} copy(f32[768,1,768]{0,2,1:T(8,128)} %convolution_bitcast_fusion.2) | data formatting | bytes 4718592 | tf_op jit(solution)/shard_map/ogn,ogs->nos/transpose | solution.py:26
  306.9 34.9 %all-gather.9.cloned.1.call-done = f32[768,1,768]{2,1,0:T(1,128)} async-done(((f32[24,1,768]{2,1,0:T(1,128)}), f32[768,1,768]{2,1,0:T(1,128)}) %all-gather.9.cloned.1.call-update) | async-done | bytes 2359312 | tf_op jit(solution)/shard_map/all_gather | solution.py:80
  341.8 3.8 fusion.6
  345.6 2.6 fusion.54
  348.2 3.5 convolution_bitcast_fusion
  351.7 6.7 %copy.9 = f32[768,1,768]{2,1,0:T(1,128)} copy(f32[768,1,768]{0,2,1:T(8,128)} %convolution_bitcast_fusion) | data formatting | bytes 4718592 | tf_op jit(solution)/shard_map/ogn,ogs->nos/transpose | solution.py:26
  358.5 122.1 %all-reduce.12.cloned.1.call-done = (f32[768,1,768]{2,1,0:T(1,128)}, f32[768,1,768]{2,1,0:T(1,128)}) async-done(((f32[768,1,768]{2,1,0:T(1,128)}, f32[768,1,768]{2,1,0:T(1,128)}), (f32[768,1,768]{2,1,0:T(1,128)}, f32[768,1,768]{2,1,0:T(1,128)})) %all-reduce.12.cloned.1.call-update) | async-done | bytes 4718608
  484.0 49.3 %all-gather.7.cloned.1.call-done = f32[768,1,768]{2,1,0:T(1,128)} async-done(((f32[24,1,768]{2,1,0:T(1,128)}), f32[768,1,768]{2,1,0:T(1,128)}) %all-gather.7.cloned.1.call-update) | async-done | bytes 2359312 | tf_op jit(solution)/shard_map/all_gather | solution.py:80
  533.3 3.7 fusion.10
  539.1 46.3 %all-gather.11.cloned.1.call-done = f32[768,1,768]{2,1,0:T(1,128)} async-done(((f32[24,1,768]{2,1,0:T(1,128)}), f32[768,1,768]{2,1,0:T(1,128)}) %all-gather.11.cloned.1.call-update) | async-done | bytes 2359312 | tf_op jit(solution)/shard_map/all_gather | solution.py:80
  585.4 3.7 fusion.2
  (38 shorter events, 14.6 us)
Async XLA Ops:
  7.2 81.5 %copy-start.4 = (f32[2,224,768]{2,1,0:T(8,128)S(1)}, f32[2,224,768]{2,1,0:T(8,128)}, u32[]{:S(2)}) copy-start(f32[2,224,768]{2,1,0:T(8,128)} %param.4) | copy-start | bytes 4128772
  7.2 81.5 %all-reduce.10.cloned.1.call-start = ((), (), s32[]{:S(2)}) async-start(), calls=%async_computation | async-start | bytes 2752512 | tf_op jit(solution)/shard_map/psum | solution.py:69
  9.6 228.0 %all-reduce.14.cloned.1.call-start = ((), (), s32[]{:S(2)}) async-start(), calls=%async_computation.6 | async-start | bytes 9437184
  111.8 0.7 copy-start.6
  111.8 178.3 %all-gather.5.cloned.1.call-start = ((), (), s32[]{:S(2)}) async-start(), calls=%async_computation.1 | async-start | bytes 2433024 | tf_op jit(solution)/shard_map/all_gather | solution.py:80
  239.2 102.6 %all-gather.9.cloned.1.call-start = ((), (), s32[]{:S(2)}) async-start(), calls=%async_computation.3 | async-start | bytes 2433024 | tf_op jit(solution)/shard_map/all_gather | solution.py:80
  242.0 238.6 %all-reduce.12.cloned.1.call-start = ((), (), s32[]{:S(2)}) async-start(), calls=%async_computation.5 | async-start | bytes 9437184
  290.2 3.8 copy-start
  341.8 3.8 copy-start.1
  358.5 174.8 %all-gather.7.cloned.1.call-start = ((), (), s32[]{:S(2)}) async-start(), calls=%async_computation.2 | async-start | bytes 2433024 | tf_op jit(solution)/shard_map/all_gather | solution.py:80
  482.2 103.3 %all-gather.11.cloned.1.call-start = ((), (), s32[]{:S(2)}) async-start(), calls=%async_computation.4 | async-start | bytes 2433024 | tf_op jit(solution)/shard_map/all_gather | solution.py:80
  533.3 3.8 copy-start.2
  585.4 3.8 copy-start.3
  589.2 2.1 copy-start.5
Sparse Core Ops, SparseCore 0:
  10.9 77.6 all-reduce.9
  112.0 125.6 all-reduce.13
  240.8 49.3 all-gather.4
  293.1 48.6 all-gather.8
  358.6 121.9 all-reduce.11
  483.9 49.3 all-gather.6
  536.7 48.6 all-gather.10
where the time goes:
time: 601 us; the launch traced here: 600 us
  waiting for transfers between devices  435 us (72%)
  blocking collectives  66.7 us (11%)
  matrix products  38.4 us (6%)
  local copies, waits for them, and re-layouts  31.8 us (5%)
  between operations  17.3 us (3%)
  other arithmetic  10.1 us (2%)
    all_gather x4, waiting for transfers between devices, spread_rows(): return lax.all_gather(shares, 'fsdp', axis=0, tiled=True)  179 us
    unnamed x9, waiting for transfers between devices  178 us
    psum x1, waiting for transfers between devices, shards(): summed = lax.psum(local_grads, 'dp')  79 us
    psum x1, blocking collectives, shards(): squares_sum = lax.psum(jnp.sum(direction * direction, axis=(1, 2)), 'fsdp')  66.7 us
    transpose x4, local copies, waits for them, and re-layouts, partial_gram(): jnp.einsum('ogn,ogs->nos', operand, operand, preferred_element_type=jnp.f...  26.9 us
    dot_general x4, matrix products, newton_schulz(): jnp.einsum('lir,rlc->lic', current, gram_whole, preferred_element_type=jn...  15 us
    dot_general x4, matrix products, partial_gram(): jnp.einsum('ogn,ogs->nos', operand, operand, preferred_element_type=jnp.f...  14.1 us
  transfers between devices with their start and end apart: 7, of which 7 were waited for; matrix products, arithmetic and copies ran while one was open for 4% of the time, Pallas kernels for 0%

commit v1 on v0

v1 whole, which is shorter than its diff:
```python
import functools
import math

import jax
import jax.numpy as jnp
from jax import lax
from jax.experimental import pallas as pl
from jax.experimental.pallas import tpu as pltpu
from jax.sharding import PartitionSpec as P

D = 7168
R = 768

QUINTIC_LINEAR = 3.4445
QUINTIC_CUBIC = -4.775
QUINTIC_FIFTH = 2.0315
MOMENTUM_FACTOR = 0.95
LEARNING_RATE = 0.02
WEIGHT_DECAY = 0.1
NORM_EPSILON = 1e-07
UPDATE_FACTOR = 0.2

MESH = pl.DeviceIdType.MESH
F32 = jnp.float32
BF16 = jnp.bfloat16
NZ = 8
CH = 56
SUB = 3
W = R // SUB
BA, BB = 48, 40
BLOCKS = 11
SPLIT = 16 * BA


def device(x, y, z, c):
    return (z, (x * 4 + y) * 2 + c)


def remote(src, dst, send, recv, target):
    return pltpu.make_async_remote_copy(
        src_ref=src, dst_ref=dst, send_sem=send, recv_sem=recv, device_id=target, device_id_type=MESH
    )


def gram_kernel(
    g_ref, m_ref, s_ref, ga, gb,
    acc, rl, rs, mbuf, dx, dh, dl, packed, ra1, rb1, ra2, rb2, share, rz, piece, gz,
    msem, ls, lr, ss, sr, als, alr, ass, asr, cs, cr,
    a1s, a1r, b1s, b1r, a2s, a2r, b2s, b2r, z1s, z1r, z2s, z2r,
    ga1s, ga1r, gb1s, gb1r, ga2s, ga2r, gb2s, gb2r, gcs, gcr,
):
    z = lax.axis_index("dp")
    f = lax.axis_index("fsdp")
    c = f % 2
    y = (f // 2) % 4
    x = f // 8
    layer = z // 4
    q = z % 4
    other = device(x, y, z, 1 - c)
    way = 1 - 2 * c
    up = device(x, y, (z + way + NZ) % NZ, c)
    down = device(x, y, (z - way + NZ) % NZ, c)

    def chunk(offset):
        return (z + way * offset + 2 * NZ) % NZ

    fetch = pltpu.make_async_copy(m_ref.at[pl.ds(pl.multiple_of(z * CH, 8), CH)], mbuf, msem)
    fetch.start()

    barrier = pltpu.get_barrier_semaphore()
    greeted = [other]
    greeted += [device(x, y, (z + o) % NZ, c) for o in range(1, NZ)]
    greeted += [device((x + o) % 4, y, z, c) for o in range(1, 4)]
    greeted += [device(x, (y + o) % 4, z, c) for o in range(1, 4)]
    for target in greeted:
        pl.semaphore_signal(barrier, inc=1, device_id=target, device_id_type=MESH)
    for i in range(4):
        rows = g_ref[i * 2 * CH : (i + 1) * 2 * CH, :].astype(F32)
        acc[2 * i] = rows[:CH]
        acc[2 * i + 1] = rows[CH:]
    pl.semaphore_wait(barrier, len(greeted))

    def cols(k):
        return pl.ds(k * W, W)

    started = []

    def go(copy):
        copy.start()
        started.append(copy)
        return copy

    def long_hop(step, k):
        return remote(acc.at[chunk(4 - step), :, cols(k)], rl.at[step, :, cols(k)], ls.at[step, k], lr.at[step, k], up)

    def short_hop(step, k):
        return remote(acc.at[chunk(step - 3), :, cols(k)], rs.at[step, :, cols(k)], ss.at[step, k], sr.at[step, k], down)

    hops = {}
    for k in range(SUB):
        hops["l", 0, k] = go(long_hop(0, k))
        hops["s", 0, k] = go(short_hop(0, k))
    for step in range(1, 4):
        for k in range(SUB):
            hops["l", step - 1, k].wait_recv()
            at = chunk(4 - step)
            acc[at, :, cols(k)] = acc[at, :, cols(k)] + rl[step - 1, :, cols(k)]
            hops["l", step, k] = go(long_hop(step, k))
            if step < 3:
                hops["s", step - 1, k].wait_recv()
                at = chunk(step - 3)
                acc[at, :, cols(k)] = acc[at, :, cols(k)] + rs[step - 1, :, cols(k)]
                hops["s", step, k] = go(short_hop(step, k))

    def gather_up(step, k):
        at = chunk(-step)
        return remote(s_ref.at[at, :, cols(k)], s_ref.at[at, :, cols(k)], als.at[step, k], alr.at[step, k], up)

    def gather_down(step, k):
        at = chunk(step)
        return remote(s_ref.at[at, :, cols(k)], s_ref.at[at, :, cols(k)], ass.at[step, k], asr.at[step, k], down)

    fetch.wait()
    mine = []
    for k in range(SUB):
        hops["s", 2, k].wait_recv()
        hops["l", 3, k].wait_recv()
        total = acc[z, :, cols(k)] + rs[2, :, cols(k)] + rl[3, :, cols(k)]
        s_ref[z, :, cols(k)] = total
        d = total + MOMENTUM_FACTOR * (MOMENTUM_FACTOR * mbuf[:, cols(k)] + total)
        dx[0:CH, cols(k)] = d
        mine.append(
            go(remote(dx.at[pl.ds(0, CH), cols(k)], dx.at[pl.ds(CH, CH), cols(k)], cs.at[k], cr.at[k], other))
        )
        hops["u", 0, k] = go(gather_up(0, k))
        hops["d", 0, k] = go(gather_down(0, k))

    for k in range(SUB):
        mine[k].wait_recv()
        d = dx[:, cols(k)]
        hi = d.astype(BF16)
        lo = (d - hi.astype(F32)).astype(BF16)
        dh[:, cols(k)] = hi
        dl[:, cols(k)] = lo
        if k == 0:
            dh[:, R : R + W] = hi
            dl[:, R : R + W] = lo

    def gram(first, second, width):
        li = pl.ds(pl.multiple_of(first * 128, 128), 128)
        ri = pl.ds(pl.multiple_of(second * 128, 128), width)

        def dot(left, right):
            return lax.dot_general(left, right, (((0,), (0,)), ((), ())), preferred_element_type=F32)

        lh, ll, rh, rlo = dh[:, li], dl[:, li], dh[:, ri], dl[:, ri]
        return dot(lh, rh) + (dot(lh, rlo) + dot(ll, rh))

    for a in range(3):
        block = gram(3 * c + a, 3 * c + a, 384)
        for k in range(3):
            packed[(3 * a + k) * 128 : (3 * a + k + 1) * 128, :] = block[:, k * 128 : (k + 1) * 128]
    for b in range(2):
        packed[(9 + b) * 128 : (10 + b) * 128, :] = gram(2 * c + b, 2 * c + b + 3, 128)

    pa = (x * (1 - c) + y * c, y * (1 - c) + x * c)
    pb = (pa[1], pa[0])

    def on_a(first, second):
        return device(first * (1 - c) + second * c, second * (1 - c) + first * c, z, c)

    def on_b(first, second):
        return on_a(second, first)

    paths = (
        (0, BA, pa, on_a, ra1, ra2, a1s, a1r, a2s, a2r, ga, ga1s, ga1r, ga2s, ga2r),
        (SPLIT, BB, pb, on_b, rb1, rb2, b1s, b1r, b2s, b2r, gb, gb1s, gb1r, gb2s, gb2r),
    )
    order = (2, 1, 3)

    first_hops = []
    for base, rows, (p1, p2), on, r1, r2, s1, t1, s2, t2, *_ in paths:
        size = 4 * rows
        for o in order:
            to = (p1 + o) % 4
            src = packed.at[pl.ds(pl.multiple_of(base + to * size, 8), size)]
            first_hops.append(go(remote(src, r1.at[o - 1], s1.at[o - 1], t1.at[o - 1], on(to, p2))))

    for k in range(SUB):
        hops["u", 0, k].wait_recv()
        hops["u", 1, k] = go(gather_up(1, k))
        hops["d", 0, k].wait_recv()
        hops["d", 1, k] = go(gather_down(1, k))

    second_hops = []
    for n, (base, rows, (p1, p2), on, r1, r2, s1, t1, s2, t2, *_) in enumerate(paths):
        size = 4 * rows
        for hop in first_hops[3 * n : 3 * n + 3]:
            hop.wait_recv()
        own = pl.ds(pl.multiple_of(base + p1 * size, 8), size)
        r1[3] = (packed[own, :] + r1[0]) + (r1[1] + r1[2])
        for o in order:
            to = (p2 + o) % 4
            src = r1.at[3, pl.ds(pl.multiple_of(to * rows, 8), rows)]
            second_hops.append(go(remote(src, r2.at[o - 1], s2.at[o - 1], t2.at[o - 1], on(p1, to))))
    for n, (base, rows, (p1, p2), on, r1, r2, *_) in enumerate(paths):
        for hop in second_hops[3 * n : 3 * n + 3]:
            hop.wait_recv()
        own = pl.ds(pl.multiple_of(p2 * rows, 8), rows)
        start = 0 if n == 0 else BA
        share[start : start + rows, :] = (r1[3, own, :] + r2[0]) + (r2[1] + r2[2])
    share[BA + BB : 96, :] = jnp.zeros((96 - BA - BB, 128), F32)

    quarter = []
    for o in (2, 1, 3):
        to = (q + o) % 4
        src = share.at[pl.ds(pl.multiple_of(to * 24, 8), 24)]
        quarter.append(go(remote(src, rz.at[o - 1], z1s.at[o - 1], z1r.at[o - 1], device(x, y, layer * 4 + to, c))))
    for hop in quarter:
        hop.wait_recv()
    at = pl.ds(pl.multiple_of(q * 24, 8), 24)
    total = (share[at, :] + rz[0]) + (rz[1] + rz[2])
    piece[...] = total
    gz[layer, at, :] = total
    spread = []
    for o in (4, 3, 5, 2, 6, 1, 7):
        spread.append(
            go(remote(piece, gz.at[layer, at], z2s.at[o - 1], z2r.at[o - 1], device(x, y, (z + o) % NZ, c)))
        )
    for hop in spread:
        hop.wait_recv()

    near, far = [], []
    for n, (base, rows, (p1, p2), on, r1, r2, s1, t1, s2, t2, out, u1, v1, u2, v2) in enumerate(paths):
        start = 0 if n == 0 else BA
        out[c, p1, p2] = gz[:, start : start + rows, :]
        block = out.at[c, p1, p2]
        for o in order:
            near.append(go(remote(block, block, u1.at[o - 1], v1.at[o - 1], on(p1, (p2 + o) % 4))))
        for o in order:
            far.append(go(remote(block, block, u2.at[o - 1, 0], v2.at[o - 1, 0], on((p1 + o) % 4, p2))))

    for k in range(SUB):
        hops["u", 1, k].wait_recv()
        hops["u", 2, k] = go(gather_up(2, k))
        hops["d", 1, k].wait_recv()
        hops["d", 2, k] = go(gather_down(2, k))

    for i, o in enumerate(order):
        for n, (base, rows, (p1, p2), on, r1, r2, s1, t1, s2, t2, out, u1, v1, u2, v2) in enumerate(paths):
            near[3 * n + i].wait_recv()
            block = out.at[c, p1, (p2 + 4 - o) % 4]
            for e in order:
                far.append(go(remote(block, block, u2.at[e - 1, o], v2.at[e - 1, o], on((p1 + e) % 4, p2))))

    for k in range(SUB):
        hops["u", 2, k].wait_recv()
        hops["u", 3, k] = go(gather_up(3, k))

    crossing = []
    for n, (base, rows, (p1, p2), on, r1, r2, s1, t1, s2, t2, out, *_) in enumerate(paths):
        block = out.at[c, p1]
        crossing.append(go(remote(block, block, gcs.at[n, 0], gcr.at[n, 0], other)))
    for i, o in enumerate(order):
        for n, (base, rows, (p1, p2), on, r1, r2, s1, t1, s2, t2, out, *_) in enumerate(paths):
            far[3 * n + i].wait_recv()
            for j in range(3):
                far[6 + 6 * j + 3 * n + i].wait_recv()
            block = out.at[c, (p1 + 4 - o) % 4]
            crossing.append(go(remote(block, block, gcs.at[n, o], gcr.at[n, o], other)))
    for hop in crossing:
        hop.wait_recv()
    for k in range(SUB):
        hops["d", 2, k].wait_recv()
        hops["u", 3, k].wait_recv()
    for copy in started:
        copy.wait_send()


def split(value):
    hi = value.astype(BF16)
    return hi, (value - hi.astype(F32)).astype(BF16)


def dot3(left, right):
    (lh, ll), (rh, rl) = left, right

    def dot(a, b):
        return jnp.dot(a, b, preferred_element_type=F32)

    return dot(lh, rh) + (dot(lh, rl) + dot(ll, rh))


def symmetric_product(out, lh, ll, rh, rl):
    for j in range(3):
        rows = slice(0, (j + 1) * 256)
        at = slice(j * 256, (j + 1) * 256)
        block = dot3((lh[rows, :], ll[rows, :]), (rh[:, at], rl[:, at]))
        out[rows, at] = block
        for i in range(j):
            out[at, i * 256 : (i + 1) * 256] = block[i * 256 : (i + 1) * 256].T


def update_kernel(s_ref, m_ref, w_ref, ga, gb, nm_ref, up_ref, nw_ref, g, a2, ah, al, ph, plo, bh, bl):
    for layer in range(2):
        trace = jnp.zeros((), F32)
        eye = lax.broadcasted_iota(jnp.int32, (128, 128), 0) == lax.broadcasted_iota(jnp.int32, (128, 128), 1)
        for h in range(2):
            rows_a = ga[h, :, layer * BA : (layer + 1) * BA, :].reshape(16 * BA, 128)
            rows_b = gb[h, :, layer * BB : (layer + 1) * BB, :].reshape(16 * BB, 128)
            for b in range(BLOCKS):
                if b < 9:
                    i = 3 * h + b // 3
                    j = (i + b % 3) % 6
                else:
                    i = 2 * h + b - 9
                    j = (i + 3) % 6
                if i == 3:
                    if j == 0:
                        continue
                block = rows_a[b * 128 : (b + 1) * 128] if b < 6 else rows_b[(b - 6) * 128 : (b - 5) * 128]
                g[i * 128 : (i + 1) * 128, j * 128 : (j + 1) * 128] = block
                if i == j:
                    trace = trace + jnp.sum(jnp.where(eye, block, 0.0))
                else:
                    g[j * 128 : (j + 1) * 128, i * 128 : (i + 1) * 128] = block.T
        inverse = 1.0 / (jnp.sqrt(jnp.broadcast_to(trace, (8, 128))) + NORM_EPSILON)
        scale = inverse[0:1, 0:1]
        a = g[...] * (scale * scale)
        g[...] = a
        ah[...], al[...] = split(a)
        symmetric_product(a2, ah, al, ah, al)
        diagonal = lax.broadcasted_iota(jnp.int32, (R, R), 0) == lax.broadcasted_iota(jnp.int32, (R, R), 1)
        p = jnp.where(diagonal, QUINTIC_LINEAR, 0.0) + QUINTIC_CUBIC * g[...] + QUINTIC_FIFTH * a2[...]
        ph[...], plo[...] = split(p)
        symmetric_product(a2, ph, plo, ah, al)
        bh[...], bl[...] = split(a2[...])
        symmetric_product(g, ph, plo, bh, bl)
        ah[...], al[...] = split(g[...])
        rows = slice(layer * 224, (layer + 1) * 224)
        summed = s_ref[rows, :]
        new_momentum = MOMENTUM_FACTOR * m_ref[rows, :] + summed
        nm_ref[rows, :] = new_momentum
        direction = summed + MOMENTUM_FACTOR * new_momentum
        x1 = dot3(split(direction), (ph[...], plo[...])) * scale
        second = (ah[...], al[...])
        y = dot3(split(x1), second)
        t = dot3(split(y), second)
        orthogonal = QUINTIC_LINEAR * x1 + QUINTIC_CUBIC * y + QUINTIC_FIFTH * t
        update = UPDATE_FACTOR * math.sqrt(max(D, R)) * orthogonal
        up_ref[rows, :] = update
        weights = w_ref[rows, :]
        nw_ref[rows, :] = weights - LEARNING_RATE * (update + WEIGHT_DECAY * weights)


def shards(replica_grads, momentum, weights):
    grads = replica_grads.reshape(NZ * CH, R)
    momentum = momentum.reshape(NZ * CH, R)
    weights = weights.reshape(NZ * CH, R)
    vmem = pl.BlockSpec(memory_space=pltpu.VMEM)
    sem = pltpu.SemaphoreType.DMA
    summed, ga, gb = pl.pallas_call(
        gram_kernel,
        out_shape=(
            jax.ShapeDtypeStruct((NZ, CH, R), F32),
            jax.ShapeDtypeStruct((2, 4, 4, 2, BA, 128), F32),
            jax.ShapeDtypeStruct((2, 4, 4, 2, BB, 128), F32),
        ),
        in_specs=[vmem, pl.BlockSpec(memory_space=pl.ANY)],
        out_specs=(vmem, vmem, vmem),
        scratch_shapes=[
            pltpu.VMEM((NZ, CH, R), F32),
            pltpu.VMEM((4, CH, R), F32),
            pltpu.VMEM((3, CH, R), F32),
            pltpu.VMEM((CH, R), F32),
            pltpu.VMEM((2 * CH, R), F32),
            pltpu.VMEM((2 * CH, R + W), BF16),
            pltpu.VMEM((2 * CH, R + W), BF16),
            pltpu.VMEM((BLOCKS * 128, 128), F32),
            pltpu.VMEM((4, 4 * BA, 128), F32),
            pltpu.VMEM((4, 4 * BB, 128), F32),
            pltpu.VMEM((3, BA, 128), F32),
            pltpu.VMEM((3, BB, 128), F32),
            pltpu.VMEM((96, 128), F32),
            pltpu.VMEM((3, 24, 128), F32),
            pltpu.VMEM((24, 128), F32),
            pltpu.VMEM((2, 96, 128), F32),
            sem,
        ]
        + [sem((4, SUB)), sem((4, SUB)), sem((3, SUB)), sem((3, SUB))] * 2
        + [sem((SUB,))] * 2
        + [sem((3,))] * 10
        + [sem((7,))] * 2
        + [sem((3,))] * 4
        + [sem((3, 4))] * 4
        + [sem((2, 4))] * 2,
        compiler_params=pltpu.CompilerParams(collective_id=0, has_side_effects=True, vmem_limit_bytes=32 << 20),
        name="gram",
    )(grads, momentum)
    summed = summed.reshape(NZ * CH, R)
    ga = ga.reshape(2, 16, 2 * BA, 128)
    gb = gb.reshape(2, 16, 2 * BB, 128)
    like = jax.ShapeDtypeStruct((NZ * CH, R), F32)
    outs = pl.pallas_call(
        update_kernel,
        out_shape=(like, like, like),
        in_specs=[vmem] * 5,
        out_specs=(vmem, vmem, vmem),
        scratch_shapes=[pltpu.VMEM((R, R), F32)] * 2 + [pltpu.VMEM((R, R), BF16)] * 6,
        compiler_params=pltpu.CompilerParams(vmem_limit_bytes=48 << 20),
        name="update",
    )(summed, momentum, weights, ga, gb)
    return tuple(o.reshape(2, 224, R) for o in outs)


def solution(mesh):
    return jax.shard_map(
        shards,
        mesh=mesh,
        in_specs=(P("dp", None, "fsdp", None), P(None, "fsdp", None), P(None, "fsdp", None)),
        out_specs=(P(None, "fsdp", None), P(None, "fsdp", None), P(None, "fsdp", None)),
        check_vma=False,
    )
```

time: 601 us -> 93.8 us (0.16)
  waiting for transfers between devices: 435 us -> 0 us
  Pallas kernels: 0 us -> 88.1 us
  blocking collectives: 66.7 us -> 0 us
  matrix products: 38.4 us -> 0 us
  local copies, waits for them, and re-layouts: 31.8 us -> 4.92 us
  between operations: 17.3 us -> 0.66 us
  other arithmetic: 10.1 us -> 0 us
    all_gather x4 -> x0, waiting for transfers between devices: 179 us -> none  [spread_rows(): return lax.all_gather(shares, 'fsdp', axis=0, tiled=True)]
    unnamed x9 -> x0, waiting for transfers between devices: 178 us -> none
    pallas_call x0 -> x2, Pallas kernels: none -> 88.1 us  [the longest x1 63.4 us: shards(): pl.pallas_call(gram_kernel, out_shape=(jax.ShapeDtypeStruct((NZ, CH, R),...]
    psum x1 -> x0, waiting for transfers between devices: 79 us -> none  [shards(): summed = lax.psum(local_grads, 'dp')]
    psum x1 -> x0, blocking collectives: 66.7 us -> none  [shards(): squares_sum = lax.psum(jnp.sum(direction * direction, axis=(1, 2)), 'fsdp')]
    dot_general x12 -> x0, matrix products: 38.4 us -> none  [the longest x4 15 us: newton_schulz(): jnp.einsum('lir,rlc->lic', current, gram_whole, preferred_element_type=jn...]
    transpose x4 -> x0, local copies, waits for them, and re-layouts: 26.9 us -> none  [partial_gram(): jnp.einsum('ogn,ogs->nos', operand, operand, preferred_element_type=jnp.f...]
  transfers between devices with their start and end apart: 7 -> 0, of which waited for: 7 -> 0; matrix products, arithmetic and copies ran while one was open for 4% -> 0% of each run, Pallas kernels for 0% -> 0%
where the time goes in v1:
time: 93.8 us; the launch traced here: 93.6 us
  Pallas kernels  88.1 us (94%)
  local copies, waits for them, and re-layouts  4.92 us (5%)
    pallas_call x1, Pallas kernels, shards(): pl.pallas_call(gram_kernel, out_shape=(jax.ShapeDtypeStruct((NZ, CH, R),...  63.4 us
    pallas_call x1, Pallas kernels, shards(): pl.pallas_call(update_kernel, out_shape=(like, like, like), in_specs=[vme...  24.6 us
    unnamed x10, local copies, waits for them, and re-layouts  4.92 us

profile of v1, /device:TPU:1, one launch (start us, length us, event | category | flops | bytes accessed | tf_op | source)
XLA Modules:
  0.0 93.6 jit_solution(17009715016408621909)
XLA Ops:
  0.6 0.0 copy-start
  0.6 1.3 %copy-done = f32[2,224,768]{2,1,0:T(8,128)S(1)} copy-done((f32[2,224,768]{2,1,0:T(8,128)S(1)}, f32[2,224,768]{2,1,0:T(8,128)}, u32[]{:S(2)}) %copy-start) | copy-done | bytes 1376280
  2.0 0.0 copy-start.4
  2.0 1.1 %copy-done.4 = bf16[1,2,224,768]{3,2,1,0:T(8,128)(2,1)S(1)} copy-done((bf16[1,2,224,768]{3,2,1,0:T(8,128)(2,1)S(1)}, bf16[1,2,224,768]{3,2,1,0:T(8,128)(2,1)}, u32[]{:S(2)}) %copy-start.4) | copy-done | bytes 688152
  3.1 0.0 copy-start.1
  3.1 63.4 %gram.1 = (f32[8,56,768]{2,1,0:T(8,128)S(1)}, f32[2,4,4,2,48,128]{5,4,3,2,1,0:T(8,128)S(1)}, f32[2,4,4,2,40,128]{5,4,3,2,1,0:T(8,128)S(1)}) custom-call(bf16[448,768]{1,0:T(8,128)(2,1)S(1)} %bitcast.15, f32[448,768]{1,0:T(8,128)S(1)} %bitcast.9), custom_call_target="tpu_custom_call" | custom-call | tf_op jit(solution)/shard_map/gram/pallas_call | solution.py:362
  66.5 0.0 copy-start.2
  66.5 1.1 %copy-done.2 = f32[2,4,4,2,48,128]{5,4,3,2,1,0:T(8,128)} copy-done((f32[2,4,4,2,48,128]{5,4,3,2,1,0:T(8,128)}, f32[2,4,4,2,48,128]{5,4,3,2,1,0:T(8,128)S(1)}, u32[]{:S(2)}) %copy-start.2) | copy-done | bytes 1572888
  67.6 0.0 copy-done.1
  67.6 0.0 copy-start.3
  67.7 1.3 %copy-done.3 = f32[2,224,768]{2,1,0:T(8,128)S(1)} copy-done((f32[2,224,768]{2,1,0:T(8,128)S(1)}, f32[2,224,768]{2,1,0:T(8,128)}, u32[]{:S(2)}) %copy-start.3) | copy-done | bytes 1376280
  69.0 24.6 %update.1 = (f32[448,768]{1,0:T(8,128)}, f32[448,768]{1,0:T(8,128)}, f32[448,768]{1,0:T(8,128)}) custom-call(f32[448,768]{1,0:T(8,128)S(1)} %bitcast.13, f32[448,768]{1,0:T(8,128)S(1)} %bitcast.10, f32[448,768]{1,0:T(8,128)S(1)} %bitcast.12, f32[2,16,96,128]{3,2,1,0:T(8,128)} %bitcast.11, f32[2,16,80,128]{3,2,1,0:T(8,128)S(1)} %bitcast.14), custom_call_target="tpu_custom_call" | custom-call | tf_op jit(solution)/shard_map/update/pallas_call | solution.py:404
Async XLA Ops:
  0.6 1.3 %copy-start = (f32[2,224,768]{2,1,0:T(8,128)S(1)}, f32[2,224,768]{2,1,0:T(8,128)}, u32[]{:S(2)}) copy-start(f32[2,224,768]{2,1,0:T(8,128)} %param.4) | copy-start | bytes 4128772
  2.0 1.1 %copy-start.4 = (bf16[1,2,224,768]{3,2,1,0:T(8,128)(2,1)S(1)}, bf16[1,2,224,768]{3,2,1,0:T(8,128)(2,1)}, u32[]{:S(2)}) copy-start(bf16[1,2,224,768]{3,2,1,0:T(8,128)(2,1)} %param.3) | copy-start | bytes 2064388
  3.1 64.6 %copy-start.1 = (f32[2,224,768]{2,1,0:T(8,128)S(1)}, f32[2,224,768]{2,1,0:T(8,128)}, u32[]{:S(2)}) copy-start(f32[2,224,768]{2,1,0:T(8,128)} %param.4) | copy-start | bytes 4128772
  66.5 1.2 %copy-start.2 = (f32[2,4,4,2,48,128]{5,4,3,2,1,0:T(8,128)}, f32[2,4,4,2,48,128]{5,4,3,2,1,0:T(8,128)S(1)}, u32[]{:S(2)}) copy-start(f32[2,4,4,2,48,128]{5,4,3,2,1,0:T(8,128)S(1)} %get-tuple-element.10) | copy-start | bytes 4718596
  67.6 1.3 %copy-start.3 = (f32[2,224,768]{2,1,0:T(8,128)S(1)}, f32[2,224,768]{2,1,0:T(8,128)}, u32[]{:S(2)}) copy-start(f32[2,224,768]{2,1,0:T(8,128)} %param.5) | copy-start | bytes 4128772

commit v2 on v1

--- a/solution.py
+++ b/solution.py
@@ -43,11 +43,12 @@
 
 
 def gram_kernel(
-    g_ref, m_ref, s_ref, ga, gb,
+    g_ref, m_ref, nm_ref, up_ref,
+    graw, s_ref, ga, gb, g, a2, ah, al, ph, plo, bh, bl, work, theirs, leave,
     acc, rl, rs, mbuf, dx, dh, dl, packed, ra1, rb1, ra2, rb2, share, rz, piece, gz,
-    msem, ls, lr, ss, sr, als, alr, ass, asr, cs, cr,
+    msem, gsem, ls, lr, ss, sr, als, alr, ass, asr, cs, cr,
     a1s, a1r, b1s, b1r, a2s, a2r, b2s, b2r, z1s, z1r, z2s, z2r,
-    ga1s, ga1r, gb1s, gb1r, ga2s, ga2r, gb2s, gb2r, gcs, gcr,
+    ga1s, ga1r, gb1s, gb1r, ga2s, ga2r, gb2s, gb2r, gcs, gcr, dsem, usem,
 ):
     z = lax.axis_index("dp")
     f = lax.axis_index("fsdp")
@@ -64,7 +65,9 @@
     def chunk(offset):
         return (z + way * offset + 2 * NZ) % NZ
 
-    fetch = pltpu.make_async_copy(m_ref.at[pl.ds(pl.multiple_of(z * CH, 8), CH)], mbuf, msem)
+    load = pltpu.make_async_copy(g_ref, graw, gsem)
+    load.start()
+    fetch = pltpu.make_async_copy(m_ref, mbuf, msem)
     fetch.start()
 
     barrier = pltpu.get_barrier_semaphore()
@@ -74,8 +77,9 @@
     greeted += [device(x, (y + o) % 4, z, c) for o in range(1, 4)]
     for target in greeted:
         pl.semaphore_signal(barrier, inc=1, device_id=target, device_id_type=MESH)
+    load.wait()
     for i in range(4):
-        rows = g_ref[i * 2 * CH : (i + 1) * 2 * CH, :].astype(F32)
+        rows = graw[i * 2 * CH : (i + 1) * 2 * CH, :].astype(F32)
         acc[2 * i] = rows[:CH]
         acc[2 * i + 1] = rows[CH:]
     pl.semaphore_wait(barrier, len(greeted))
@@ -127,7 +131,7 @@
         hops["l", 3, k].wait_recv()
         total = acc[z, :, cols(k)] + rs[2, :, cols(k)] + rl[3, :, cols(k)]
         s_ref[z, :, cols(k)] = total
-        d = total + MOMENTUM_FACTOR * (MOMENTUM_FACTOR * mbuf[:, cols(k)] + total)
+        d = total + MOMENTUM_FACTOR * (MOMENTUM_FACTOR * mbuf[z, :, cols(k)] + total)
         dx[0:CH, cols(k)] = d
         mine.append(
             go(remote(dx.at[pl.ds(0, CH), cols(k)], dx.at[pl.ds(CH, CH), cols(k)], cs.at[k], cr.at[k], other))
@@ -258,21 +262,81 @@
         hops["u", 3, k] = go(gather_up(3, k))
 
     crossing = []
-    for n, (base, rows, (p1, p2), on, r1, r2, s1, t1, s2, t2, out, *_) in enumerate(paths):
-        block = out.at[c, p1]
-        crossing.append(go(remote(block, block, gcs.at[n, 0], gcr.at[n, 0], other)))
+
+    def cross(n, first, o):
+        out = (ga, gb)[n]
+        block = out.at[c, first, :, 1 - c]
+        crossing.append(go(remote(block, block, gcs.at[n, o], gcr.at[n, o], other)))
+
+    for n in range(2):
+        cross(n, paths[n][2][0], 0)
     for i, o in enumerate(order):
-        for n, (base, rows, (p1, p2), on, r1, r2, s1, t1, s2, t2, out, *_) in enumerate(paths):
+        for n in range(2):
             far[3 * n + i].wait_recv()
             for j in range(3):
                 far[6 + 6 * j + 3 * n + i].wait_recv()
-            block = out.at[c, (p1 + 4 - o) % 4]
-            crossing.append(go(remote(block, block, gcs.at[n, o], gcr.at[n, o], other)))
+            cross(n, (paths[n][2][0] + 4 - o) % 4, o)
     for hop in crossing:
         hop.wait_recv()
+
+    trace = jnp.zeros((), F32)
+    eye = lax.broadcasted_iota(jnp.int32, (128, 128), 0) == lax.broadcasted_iota(jnp.int32, (128, 128), 1)
+    for h in range(2):
+        rows_a = ga[h, :, :, c].reshape(16 * BA, 128)
+        rows_b = gb[h, :, :, c].reshape(16 * BB, 128)
+        for b in range(BLOCKS):
+            if b < 9:
+                i = 3 * h + b // 3
+                j = (i + b % 3) % 6
+            else:
+                i = 2 * h + b - 9
+                j = (i + 3) % 6
+            if i == 3 and j == 0:
+                continue
+            block = rows_a[b * 128 : (b + 1) * 128] if b < 6 else rows_b[(b - 6) * 128 : (b - 5) * 128]
+            g[i * 128 : (i + 1) * 128, j * 128 : (j + 1) * 128] = block
+            if i == j:
+                trace = trace + jnp.sum(jnp.where(eye, block, 0.0))
+            else:
+                g[j * 128 : (j + 1) * 128, i * 128 : (i + 1) * 128] = block.T
+    inverse = 1.0 / (jnp.sqrt(jnp.broadcast_to(trace, (8, 128))) + NORM_EPSILON)
+    scale = inverse[0:1, 0:1]
+    a = g[...] * (scale * scale)
+    g[...] = a
+    ah[...], al[...] = split(a)
+    symmetric_product(a2, ah, al, ah, al)
+
     for k in range(SUB):
         hops["d", 2, k].wait_recv()
         hops["u", 3, k].wait_recv()
+    for i in range(NZ):
+        nm_ref[i] = MOMENTUM_FACTOR * mbuf[i] + s_ref[i]
+    for i in range(4):
+        at = 4 * (1 - c) + i
+        leave[i * CH : (i + 1) * CH, :] = s_ref[at] + MOMENTUM_FACTOR * nm_ref[at]
+    handed = go(remote(leave, work.at[pl.ds(224, 224)], dsem.at[0], dsem.at[1], other))
+    for i in range(4):
+        at = 4 * c + i
+        work[i * CH : (i + 1) * CH, :] = s_ref[at] + MOMENTUM_FACTOR * nm_ref[at]
+
+    diagonal = lax.broadcasted_iota(jnp.int32, (R, R), 0) == lax.broadcasted_iota(jnp.int32, (R, R), 1)
+    p = jnp.where(diagonal, QUINTIC_LINEAR, 0.0) + QUINTIC_CUBIC * g[...] + QUINTIC_FIFTH * a2[...]
+    ph[...], plo[...] = split(p)
+    symmetric_product(a2, ph, plo, ah, al)
+    bh[...], bl[...] = split(a2[...])
+    symmetric_product(g, ph, plo, bh, bl)
+    ah[...], al[...] = split(g[...])
+
+    handed.wait_recv()
+    x1 = dot3(split(work[...]), (ph[...], plo[...])) * scale
+    second = (ah[...], al[...])
+    y1 = dot3(split(x1), second)
+    partial = QUINTIC_LINEAR * x1 + QUINTIC_CUBIC * y1
+    factor = UPDATE_FACTOR * math.sqrt(max(D, R))
+    theirs[...] = factor * (partial[224:] + QUINTIC_FIFTH * dot3(split(y1[224:]), second))
+    back = go(remote(theirs, up_ref.at[c], usem.at[0], usem.at[1], other))
+    up_ref[c] = factor * (partial[:224] + QUINTIC_FIFTH * dot3(split(y1[:224]), second))
+    back.wait_recv()
     for copy in started:
         copy.wait_send()
 
@@ -301,78 +365,50 @@
             out[at, i * 256 : (i + 1) * 256] = block[i * 256 : (i + 1) * 256].T
 
 
-def update_kernel(s_ref, m_ref, w_ref, ga, gb, nm_ref, up_ref, nw_ref, g, a2, ah, al, ph, plo, bh, bl):
-    for layer in range(2):
-        trace = jnp.zeros((), F32)
-        eye = lax.broadcasted_iota(jnp.int32, (128, 128), 0) == lax.broadcasted_iota(jnp.int32, (128, 128), 1)
-        for h in range(2):
-            rows_a = ga[h, :, layer * BA : (layer + 1) * BA, :].reshape(16 * BA, 128)
-            rows_b = gb[h, :, layer * BB : (layer + 1) * BB, :].reshape(16 * BB, 128)
-            for b in range(BLOCKS):
-                if b < 9:
-                    i = 3 * h + b // 3
-                    j = (i + b % 3) % 6
-                else:
-                    i = 2 * h + b - 9
-                    j = (i + 3) % 6
-                if i == 3:
-                    if j == 0:
-                        continue
-                block = rows_a[b * 128 : (b + 1) * 128] if b < 6 else rows_b[(b - 6) * 128 : (b - 5) * 128]
-                g[i * 128 : (i + 1) * 128, j * 128 : (j + 1) * 128] = block
-                if i == j:
-                    trace = trace + jnp.sum(jnp.where(eye, block, 0.0))
-                else:
-                    g[j * 128 : (j + 1) * 128, i * 128 : (i + 1) * 128] = block.T
-        inverse = 1.0 / (jnp.sqrt(jnp.broadcast_to(trace, (8, 128))) + NORM_EPSILON)
-        scale = inverse[0:1, 0:1]
-        a = g[...] * (scale * scale)
-        g[...] = a
-        ah[...], al[...] = split(a)
-        symmetric_product(a2, ah, al, ah, al)
-        diagonal = lax.broadcasted_iota(jnp.int32, (R, R), 0) == lax.broadcasted_iota(jnp.int32, (R, R), 1)
-        p = jnp.where(diagonal, QUINTIC_LINEAR, 0.0) + QUINTIC_CUBIC * g[...] + QUINTIC_FIFTH * a2[...]
-        ph[...], plo[...] = split(p)
-        symmetric_product(a2, ph, plo, ah, al)
-        bh[...], bl[...] = split(a2[...])
-        symmetric_product(g, ph, plo, bh, bl)
-        ah[...], al[...] = split(g[...])
-        rows = slice(layer * 224, (layer + 1) * 224)
-        summed = s_ref[rows, :]
-        new_momentum = MOMENTUM_FACTOR * m_ref[rows, :] + summed
-        nm_ref[rows, :] = new_momentum
-        direction = summed + MOMENTUM_FACTOR * new_momentum
-        x1 = dot3(split(direction), (ph[...], plo[...])) * scale
-        second = (ah[...], al[...])
-        y = dot3(split(x1), second)
-        t = dot3(split(y), second)
-        orthogonal = QUINTIC_LINEAR * x1 + QUINTIC_CUBIC * y + QUINTIC_FIFTH * t
-        update = UPDATE_FACTOR * math.sqrt(max(D, R)) * orthogonal
-        up_ref[rows, :] = update
+def update_kernel(nm_ref, up_ref, w_ref, nm_out, up_out, nw_out, nw, sems):
+    copies = [pltpu.make_async_copy(nm_ref, nm_out, sems.at[0]), pltpu.make_async_copy(up_ref, up_out, sems.at[1])]
+    for copy in copies:
+        copy.start()
+    for i in range(4):
+        rows = pl.ds(i * 112, 112)
         weights = w_ref[rows, :]
-        nw_ref[rows, :] = weights - LEARNING_RATE * (update + WEIGHT_DECAY * weights)
+        nw[rows, :] = weights - LEARNING_RATE * (up_ref[rows, :] + WEIGHT_DECAY * weights)
+        copies.append(pltpu.make_async_copy(nw.at[rows], nw_out.at[rows], sems.at[2 + i]))
+        copies[-1].start()
+    for copy in copies:
+        copy.wait()
 
 
 def shards(replica_grads, momentum, weights):
     grads = replica_grads.reshape(NZ * CH, R)
-    momentum = momentum.reshape(NZ * CH, R)
+    momentum = momentum.reshape(NZ, CH, R)
     weights = weights.reshape(NZ * CH, R)
     vmem = pl.BlockSpec(memory_space=pltpu.VMEM)
+    hbm = pl.BlockSpec(memory_space=pltpu.HBM)
     sem = pltpu.SemaphoreType.DMA
-    summed, ga, gb = pl.pallas_call(
+    square = pltpu.VMEM((R, R), F32)
+    half = pltpu.VMEM((R, R), BF16)
+    new_momentum, update = pl.pallas_call(
         gram_kernel,
         out_shape=(
             jax.ShapeDtypeStruct((NZ, CH, R), F32),
-            jax.ShapeDtypeStruct((2, 4, 4, 2, BA, 128), F32),
-            jax.ShapeDtypeStruct((2, 4, 4, 2, BB, 128), F32),
+            jax.ShapeDtypeStruct((2, 224, R), F32),
         ),
-        in_specs=[vmem, pl.BlockSpec(memory_space=pl.ANY)],
-        out_specs=(vmem, vmem, vmem),
+        in_specs=[hbm, hbm],
+        out_specs=(vmem, vmem),
         scratch_shapes=[
+            pltpu.VMEM((NZ * CH, R), BF16),
+            pltpu.VMEM((NZ, CH, R), F32),
+            pltpu.VMEM((2, 4, 4, 2, BA, 128), F32),
+            pltpu.VMEM((2, 4, 4, 2, BB, 128), F32),
+            square, square, half, half, half, half, half, half,
+            pltpu.VMEM((NZ * CH, R), F32),
+            pltpu.VMEM((224, R), F32),
+            pltpu.VMEM((224, R), F32),
             pltpu.VMEM((NZ, CH, R), F32),
             pltpu.VMEM((4, CH, R), F32),
             pltpu.VMEM((3, CH, R), F32),
-            pltpu.VMEM((CH, R), F32),
+            pltpu.VMEM((NZ, CH, R), F32),
             pltpu.VMEM((2 * CH, R), F32),
             pltpu.VMEM((2 * CH, R + W), BF16),
             pltpu.VMEM((2 * CH, R + W), BF16),
@@ -386,6 +422,7 @@
             pltpu.VMEM((24, 128), F32),
             pltpu.VMEM((2, 96, 128), F32),
             sem,
+            sem,
         ]
         + [sem((4, SUB)), sem((4, SUB)), sem((3, SUB)), sem((3, SUB))] * 2
         + [sem((SUB,))] * 2
@@ -393,23 +430,21 @@
         + [sem((7,))] * 2
         + [sem((3,))] * 4
         + [sem((3, 4))] * 4
-        + [sem((2, 4))] * 2,
-        compiler_params=pltpu.CompilerParams(collective_id=0, has_side_effects=True, vmem_limit_bytes=32 << 20),
+        + [sem((2, 4))] * 2
+        + [sem((2,))] * 2,
+        compiler_params=pltpu.CompilerParams(collective_id=0, has_side_effects=True, vmem_limit_bytes=34 << 20),
         name="gram",
     )(grads, momentum)
-    summed = summed.reshape(NZ * CH, R)
-    ga = ga.reshape(2, 16, 2 * BA, 128)
-    gb = gb.reshape(2, 16, 2 * BB, 128)
     like = jax.ShapeDtypeStruct((NZ * CH, R), F32)
     outs = pl.pallas_call(
         update_kernel,
         out_shape=(like, like, like),
-        in_specs=[vmem] * 5,
-        out_specs=(vmem, vmem, vmem),
-        scratch_shapes=[pltpu.VMEM((R, R), F32)] * 2 + [pltpu.VMEM((R, R), BF16)] * 6,
-        compiler_params=pltpu.CompilerParams(vmem_limit_bytes=48 << 20),
+        in_specs=[vmem] * 3,
+        out_specs=(hbm, hbm, hbm),
+        scratch_shapes=[pltpu.VMEM((NZ * CH, R), F32), sem((6,))],
+        compiler_params=pltpu.CompilerParams(vmem_limit_bytes=4 << 20),
         name="update",
-    )(summed, momentum, weights, ga, gb)
+    )(new_momentum.reshape(NZ * CH, R), update.reshape(NZ * CH, R), weights)
     return tuple(o.reshape(2, 224, R) for o in outs)
 
 

time: 93.8 us -> 86.7 us (0.924)
  Pallas kernels: 88.1 us -> 83.3 us
  local copies, waits for them, and re-layouts: 4.92 us -> 2.54 us
    pallas_call x1, Pallas kernels: 24.6 us -> 2.03 us  [shards(): pl.pallas_call(update_kernel, out_shape=(like, like, like), in_specs=[vme...]
    pallas_call x1, Pallas kernels: 63.4 us -> 81.3 us  [shards(): pl.pallas_call(gram_kernel, out_shape=(jax.ShapeDtypeStruct((NZ, CH, R),...]
    unnamed x10 -> x6, local copies, waits for them, and re-layouts: 4.92 us -> 2.54 us
where the time goes in v2:
time: 86.7 us; the launch traced here: 86.5 us
  Pallas kernels  83.3 us (96%)
  local copies, waits for them, and re-layouts  2.54 us (3%)
    pallas_call x1, Pallas kernels, shards(): pl.pallas_call(gram_kernel, out_shape=(jax.ShapeDtypeStruct((NZ, CH, R),...  81.3 us
    unnamed x6, local copies, waits for them, and re-layouts  2.54 us
    pallas_call x1, Pallas kernels, shards(): pl.pallas_call(update_kernel, out_shape=(like, like, like), in_specs=[vme...  2.03 us

profile of v2, /device:TPU:1, one launch (start us, length us, event | category | flops | bytes accessed | tf_op | source)
XLA Modules:
  0.0 86.5 jit_solution(10978999737183553153)
XLA Ops:
  0.6 0.0 copy-start
  0.6 0.0 copy-start.1
  0.7 1.4 %copy-done.1 = f32[2,224,768]{2,1,0:T(8,128)S(1)} copy-done((f32[2,224,768]{2,1,0:T(8,128)S(1)}, f32[2,224,768]{2,1,0:T(8,128)}, u32[]{:S(2)}) %copy-start.1) | copy-done | bytes 1376280
  2.1 0.0 copy-start.2
  2.1 1.1 %copy-done.2 = bf16[1,2,224,768]{3,2,1,0:T(8,128)(2,1)S(1)} copy-done((bf16[1,2,224,768]{3,2,1,0:T(8,128)(2,1)S(1)}, bf16[1,2,224,768]{3,2,1,0:T(8,128)(2,1)}, u32[]{:S(2)}) %copy-start.2) | copy-done | bytes 688152
  3.2 81.3 %gram.1 = (f32[8,56,768]{2,1,0:T(8,128)S(1)}, f32[2,224,768]{2,1,0:T(8,128)S(1)}) custom-call(bf16[448,768]{1,0:T(8,128)(2,1)S(1)} %bitcast.12, f32[8,56,768]{2,1,0:T(8,128)S(1)} %bitcast.11), custom_call_target="tpu_custom_call" | custom-call | tf_op jit(solution)/shard_map/gram/pallas_call | solution.py:391
  84.5 0.0 copy-done
  84.5 2.0 %update.1 = (f32[448,768]{1,0:T(8,128)}, f32[448,768]{1,0:T(8,128)}, f32[448,768]{1,0:T(8,128)}) custom-call(f32[448,768]{1,0:T(8,128)S(1)} %bitcast.9, f32[448,768]{1,0:T(8,128)S(1)} %bitcast.10, f32[448,768]{1,0:T(8,128)S(1)} %bitcast.8), custom_call_target="tpu_custom_call" | custom-call | tf_op jit(solution)/shard_map/update/pallas_call | solution.py:439
Async XLA Ops:
  0.6 83.9 %copy-start = (f32[2,224,768]{2,1,0:T(8,128)S(1)}, f32[2,224,768]{2,1,0:T(8,128)}, u32[]{:S(2)}) copy-start(f32[2,224,768]{2,1,0:T(8,128)} %param.5) | copy-start | bytes 4128772
  0.6 1.4 %copy-start.1 = (f32[2,224,768]{2,1,0:T(8,128)S(1)}, f32[2,224,768]{2,1,0:T(8,128)}, u32[]{:S(2)}) copy-start(f32[2,224,768]{2,1,0:T(8,128)} %param.4) | copy-start | bytes 4128772
  2.1 1.1 %copy-start.2 = (bf16[1,2,224,768]{3,2,1,0:T(8,128)(2,1)S(1)}, bf16[1,2,224,768]{3,2,1,0:T(8,128)(2,1)}, u32[]{:S(2)}) copy-start(bf16[1,2,224,768]{3,2,1,0:T(8,128)(2,1)} %param.3) | copy-start | bytes 2064388

commit v3 on v2

--- a/solution.py
+++ b/solution.py
@@ -44,11 +44,11 @@
 
 def gram_kernel(
     g_ref, m_ref, nm_ref, up_ref,
-    graw, s_ref, ga, gb, g, a2, ah, al, ph, plo, bh, bl, work, theirs, leave,
+    graw, s_ref, ga, gb, g, ah, al, ph, plo, bh, bl, wh, wl, xh, xl, work, theirs, leave,
     acc, rl, rs, mbuf, dx, dh, dl, packed, ra1, rb1, ra2, rb2, share, rz, piece, gz,
     msem, gsem, ls, lr, ss, sr, als, alr, ass, asr, cs, cr,
     a1s, a1r, b1s, b1r, a2s, a2r, b2s, b2r, z1s, z1r, z2s, z2r,
-    ga1s, ga1r, gb1s, gb1r, ga2s, ga2r, gb2s, gb2r, gcs, gcr, dsem, usem,
+    ga1s, ga1r, gb1s, gb1r, ga2s, ga2r, gb2s, gb2r, gcs, gcr, dsem, usem, ready,
 ):
     z = lax.axis_index("dp")
     f = lax.axis_index("fsdp")
@@ -72,9 +72,9 @@
 
     barrier = pltpu.get_barrier_semaphore()
     greeted = [other]
-    greeted += [device(x, y, (z + o) % NZ, c) for o in range(1, NZ)]
-    greeted += [device((x + o) % 4, y, z, c) for o in range(1, 4)]
-    greeted += [device(x, (y + o) % 4, z, c) for o in range(1, 4)]
+    greeted += [device(x, y, (z + o) % NZ, c) for o in (1, NZ - 1)]
+    beside = [device((x + o) % 4, y, z, c) for o in (1, 3)] + [device(x, (y + o) % 4, z, c) for o in (1, 3)]
+    greeted += beside
     for target in greeted:
         pl.semaphore_signal(barrier, inc=1, device_id=target, device_id_type=MESH)
     load.wait()
@@ -83,6 +83,8 @@
         acc[2 * i] = rows[:CH]
         acc[2 * i + 1] = rows[CH:]
     pl.semaphore_wait(barrier, len(greeted))
+    for target in beside:
+        pl.semaphore_signal(ready, inc=1, device_id=target, device_id_type=MESH)
 
     def cols(k):
         return pl.ds(k * W, W)
@@ -160,12 +162,13 @@
         lh, ll, rh, rlo = dh[:, li], dl[:, li], dh[:, ri], dl[:, ri]
         return dot(lh, rh) + (dot(lh, rlo) + dot(ll, rh))
 
-    for a in range(3):
+    def row_blocks(a):
         block = gram(3 * c + a, 3 * c + a, 384)
         for k in range(3):
             packed[(3 * a + k) * 128 : (3 * a + k + 1) * 128, :] = block[:, k * 128 : (k + 1) * 128]
-    for b in range(2):
-        packed[(9 + b) * 128 : (10 + b) * 128, :] = gram(2 * c + b, 2 * c + b + 3, 128)
+
+    row_blocks(0)
+    row_blocks(1)
 
     pa = (x * (1 - c) + y * c, y * (1 - c) + x * c)
     pb = (pa[1], pa[0])
@@ -183,12 +186,20 @@
     order = (2, 1, 3)
 
     first_hops = []
-    for base, rows, (p1, p2), on, r1, r2, s1, t1, s2, t2, *_ in paths:
+
+    def start_first(base, rows, at, on, r1, r2, s1, t1, *_):
         size = 4 * rows
         for o in order:
-            to = (p1 + o) % 4
+            to = (at[0] + o) % 4
             src = packed.at[pl.ds(pl.multiple_of(base + to * size, 8), size)]
-            first_hops.append(go(remote(src, r1.at[o - 1], s1.at[o - 1], t1.at[o - 1], on(to, p2))))
+            first_hops.append(go(remote(src, r1.at[o - 1], s1.at[o - 1], t1.at[o - 1], on(to, at[1]))))
+
+    pl.semaphore_wait(ready, len(beside))
+    start_first(*paths[0])
+    row_blocks(2)
+    for b in range(2):
+        packed[(9 + b) * 128 : (10 + b) * 128, :] = gram(2 * c + b, 2 * c + b + 3, 128)
+    start_first(*paths[1])
 
     for k in range(SUB):
         hops["u", 0, k].wait_recv()
@@ -226,16 +237,20 @@
     total = (share[at, :] + rz[0]) + (rz[1] + rz[2])
     piece[...] = total
     gz[layer, at, :] = total
-    spread = []
     for o in (4, 3, 5, 2, 6, 1, 7):
-        spread.append(
-            go(remote(piece, gz.at[layer, at], z2s.at[o - 1], z2r.at[o - 1], device(x, y, (z + o) % NZ, c)))
-        )
-    for hop in spread:
-        hop.wait_recv()
+        go(remote(piece, gz.at[layer, at], z2s.at[o - 1], z2r.at[z], device(x, y, (z + o) % NZ, c)))
 
     near, far = [], []
-    for n, (base, rows, (p1, p2), on, r1, r2, s1, t1, s2, t2, out, u1, v1, u2, v2) in enumerate(paths):
+
+    def start_gather(n, base, rows, at, on, r1, r2, s1, t1, s2, t2, out, u1, v1, u2, v2):
+        for plane in (2 * n, 2 * n + 1, 2 * n + 4, 2 * n + 5):
+
+            @pl.when(z != plane)
+            def _():
+                land = gz.at[plane // 4, pl.ds(plane % 4 * 24, 24)]
+                remote(piece, land, z2s.at[0], z2r.at[plane], other).wait_recv()
+
+        p1, p2 = at
         start = 0 if n == 0 else BA
         out[c, p1, p2] = gz[:, start : start + rows, :]
         block = out.at[c, p1, p2]
@@ -243,6 +258,9 @@
             near.append(go(remote(block, block, u1.at[o - 1], v1.at[o - 1], on(p1, (p2 + o) % 4))))
         for o in order:
             far.append(go(remote(block, block, u2.at[o - 1, 0], v2.at[o - 1, 0], on((p1 + o) % 4, p2))))
+
+    for n in range(2):
+        start_gather(n, *paths[n])
 
     for k in range(SUB):
         hops["u", 1, k].wait_recv()
@@ -301,10 +319,17 @@
                 g[j * 128 : (j + 1) * 128, i * 128 : (i + 1) * 128] = block.T
     inverse = 1.0 / (jnp.sqrt(jnp.broadcast_to(trace, (8, 128))) + NORM_EPSILON)
     scale = inverse[0:1, 0:1]
-    a = g[...] * (scale * scale)
-    g[...] = a
-    ah[...], al[...] = split(a)
-    symmetric_product(a2, ah, al, ah, al)
+    square = scale * scale
+    for j in range(3):
+        put(ah, al, slice(0, R), COLS[j], g[:, COLS[j]] * square)
+    corner = lax.broadcasted_iota(jnp.int32, (256, 256), 0) == lax.broadcasted_iota(jnp.int32, (256, 256), 1)
+    linear = jnp.where(corner, QUINTIC_LINEAR, 0.0)
+
+    def polynomial(value, i, j):
+        value = (QUINTIC_CUBIC * square) * g[COLS[i], COLS[j]] + QUINTIC_FIFTH * value
+        return linear + value if i == j else value
+
+    symmetric_product((ah, al), (ah, al), (ph, plo), polynomial)
 
     for k in range(SUB):
         hops["d", 2, k].wait_recv()
@@ -319,33 +344,35 @@
         at = 4 * c + i
         work[i * CH : (i + 1) * CH, :] = s_ref[at] + MOMENTUM_FACTOR * nm_ref[at]
 
-    diagonal = lax.broadcasted_iota(jnp.int32, (R, R), 0) == lax.broadcasted_iota(jnp.int32, (R, R), 1)
-    p = jnp.where(diagonal, QUINTIC_LINEAR, 0.0) + QUINTIC_CUBIC * g[...] + QUINTIC_FIFTH * a2[...]
-    ph[...], plo[...] = split(p)
-    symmetric_product(a2, ph, plo, ah, al)
-    bh[...], bl[...] = split(a2[...])
-    symmetric_product(g, ph, plo, bh, bl)
-    ah[...], al[...] = split(g[...])
+    symmetric_product((ph, plo), (ah, al), (bh, bl))
+    symmetric_product((ph, plo), (bh, bl), (ah, al))
 
     handed.wait_recv()
-    x1 = dot3(split(work[...]), (ph[...], plo[...])) * scale
-    second = (ah[...], al[...])
-    y1 = dot3(split(x1), second)
-    partial = QUINTIC_LINEAR * x1 + QUINTIC_CUBIC * y1
     factor = UPDATE_FACTOR * math.sqrt(max(D, R))
-    theirs[...] = factor * (partial[224:] + QUINTIC_FIFTH * dot3(split(y1[224:]), second))
+    halves = (slice(224, 448), slice(0, 224))
+    every = slice(0, R)
+    for rows in halves:
+        put(wh, wl, rows, every, work[rows, :])
+    for rows in halves:
+        x1 = dot3((wh[rows, :], wl[rows, :]), (ph[...], plo[...])) * scale
+        work[rows, :] = QUINTIC_LINEAR * x1
+        put(xh, xl, rows, every, x1)
+    for rows in halves:
+        y1 = dot3((xh[rows, :], xl[rows, :]), (ah[...], al[...]))
+        work[rows, :] = work[rows, :] + QUINTIC_CUBIC * y1
+        put(wh, wl, rows, every, y1)
+
+    def finish(rows):
+        return factor * (work[rows, :] + QUINTIC_FIFTH * dot3((wh[rows, :], wl[rows, :]), (ah[...], al[...])))
+
+    theirs[...] = finish(halves[0])
     back = go(remote(theirs, up_ref.at[c], usem.at[0], usem.at[1], other))
-    up_ref[c] = factor * (partial[:224] + QUINTIC_FIFTH * dot3(split(y1[:224]), second))
+    up_ref[c] = finish(halves[1])
     back.wait_recv()
     for copy in started:
         copy.wait_send()
 
 
-def split(value):
-    hi = value.astype(BF16)
-    return hi, (value - hi.astype(F32)).astype(BF16)
-
-
 def dot3(left, right):
     (lh, ll), (rh, rl) = left, right
 
@@ -355,14 +382,27 @@
     return dot(lh, rh) + (dot(lh, rl) + dot(ll, rh))
 
 
-def symmetric_product(out, lh, ll, rh, rl):
+def put(hi_ref, lo_ref, rows, cols, value):
+    hi = value.astype(BF16)
+    hi_ref[rows, cols] = hi
+    lo_ref[rows, cols] = (value - hi.astype(F32)).astype(BF16)
+
+
+COLS = [slice(j * 256, (j + 1) * 256) for j in range(3)]
+
+
+def symmetric_product(left, right, out, then=None):
+    (lh, ll), (rh, rl) = left, right
     for j in range(3):
         rows = slice(0, (j + 1) * 256)
-        at = slice(j * 256, (j + 1) * 256)
-        block = dot3((lh[rows, :], ll[rows, :]), (rh[:, at], rl[:, at]))
-        out[rows, at] = block
-        for i in range(j):
-            out[at, i * 256 : (i + 1) * 256] = block[i * 256 : (i + 1) * 256].T
+        block = dot3((lh[rows, :], ll[rows, :]), (rh[:, COLS[j]], rl[:, COLS[j]]))
+        for i in range(j + 1):
+            value = block[COLS[i]]
+            if then is not None:
+                value = then(value, i, j)
+            put(*out, COLS[i], COLS[j], value)
+            if i < j:
+                put(*out, COLS[j], COLS[i], value.T)
 
 
 def update_kernel(nm_ref, up_ref, w_ref, nm_out, up_out, nw_out, nw, sems):
@@ -380,13 +420,13 @@
 
 
 def shards(replica_grads, momentum, weights):
-    grads = replica_grads.reshape(NZ * CH, R)
-    momentum = momentum.reshape(NZ, CH, R)
+    grads = pltpu.with_memory_space_constraint(replica_grads.reshape(NZ * CH, R), pltpu.HBM)
+    momentum = pltpu.with_memory_space_constraint(momentum.reshape(NZ, CH, R), pltpu.HBM)
     weights = weights.reshape(NZ * CH, R)
     vmem = pl.BlockSpec(memory_space=pltpu.VMEM)
     hbm = pl.BlockSpec(memory_space=pltpu.HBM)
     sem = pltpu.SemaphoreType.DMA
-    square = pltpu.VMEM((R, R), F32)
+    rows = pltpu.VMEM((NZ * CH, R), BF16)
     half = pltpu.VMEM((R, R), BF16)
     new_momentum, update = pl.pallas_call(
         gram_kernel,
@@ -401,7 +441,7 @@
             pltpu.VMEM((NZ, CH, R), F32),
             pltpu.VMEM((2, 4, 4, 2, BA, 128), F32),
             pltpu.VMEM((2, 4, 4, 2, BB, 128), F32),
-            square, square, half, half, half, half, half, half,
+            pltpu.VMEM((R, R), F32), half, half, half, half, half, half, rows, rows, rows, rows,
             pltpu.VMEM((NZ * CH, R), F32),
             pltpu.VMEM((224, R), F32),
             pltpu.VMEM((224, R), F32),
@@ -427,11 +467,12 @@
         + [sem((4, SUB)), sem((4, SUB)), sem((3, SUB)), sem((3, SUB))] * 2
         + [sem((SUB,))] * 2
         + [sem((3,))] * 10
-        + [sem((7,))] * 2
+        + [sem((8,))] * 2
         + [sem((3,))] * 4
         + [sem((3, 4))] * 4
         + [sem((2, 4))] * 2
-        + [sem((2,))] * 2,
+        + [sem((2,))] * 2
+        + [pltpu.SemaphoreType.REGULAR],
         compiler_params=pltpu.CompilerParams(collective_id=0, has_side_effects=True, vmem_limit_bytes=34 << 20),
         name="gram",
     )(grads, momentum)

time: 86.7 us -> 79.4 us (0.916)
  Pallas kernels: 83.3 us -> 78.7 us
  local copies, waits for them, and re-layouts: 2.54 us -> 0.01 us
    pallas_call x1, Pallas kernels: 81.3 us -> 76.7 us  [shards(): pl.pallas_call(gram_kernel, out_shape=(jax.ShapeDtypeStruct((NZ, CH, R),...]
    unnamed x6 -> x2, local copies, waits for them, and re-layouts: 2.54 us -> 0.01 us
where the time goes in v3:
time: 79.4 us; the launch traced here: 79.3 us
  Pallas kernels  78.7 us (99%)
    pallas_call x1, Pallas kernels, shards(): pl.pallas_call(gram_kernel, out_shape=(jax.ShapeDtypeStruct((NZ, CH, R),...  76.7 us
    pallas_call x1, Pallas kernels, shards(): pl.pallas_call(update_kernel, out_shape=(like, like, like), in_specs=[vme...  2.03 us

profile of v3, /device:TPU:1, one launch (start us, length us, event | category | flops | bytes accessed | tf_op | source)
XLA Modules:
  0.0 79.3 jit_solution(5450274010158941308)
XLA Ops:
  0.6 0.0 copy-start
  0.6 76.7 %gram.1 = (f32[8,56,768]{2,1,0:T(8,128)S(1)}, f32[2,224,768]{2,1,0:T(8,128)S(1)}) custom-call(bf16[448,768]{1,0:T(8,128)(2,1)} %bitcast.12, f32[8,56,768]{2,1,0:T(8,128)} %bitcast.11), custom_call_target="tpu_custom_call" | custom-call | tf_op jit(solution)/shard_map/gram/pallas_call | solution.py:431
  77.3 0.0 copy-done
  77.3 2.0 %update.1 = (f32[448,768]{1,0:T(8,128)}, f32[448,768]{1,0:T(8,128)}, f32[448,768]{1,0:T(8,128)}) custom-call(f32[448,768]{1,0:T(8,128)S(1)} %bitcast.9, f32[448,768]{1,0:T(8,128)S(1)} %bitcast.10, f32[448,768]{1,0:T(8,128)S(1)} %bitcast.8), custom_call_target="tpu_custom_call" | custom-call | tf_op jit(solution)/shard_map/update/pallas_call | solution.py:480
Async XLA Ops:
  0.6 76.7 %copy-start = (f32[2,224,768]{2,1,0:T(8,128)S(1)}, f32[2,224,768]{2,1,0:T(8,128)}, u32[]{:S(2)}) copy-start(f32[2,224,768]{2,1,0:T(8,128)} %param.5) | copy-start | bytes 4128772

commit v4 on v3

--- a/solution.py
+++ b/solution.py
@@ -44,11 +44,11 @@
 
 def gram_kernel(
     g_ref, m_ref, nm_ref, up_ref,
-    graw, s_ref, ga, gb, g, ah, al, ph, plo, bh, bl, wh, wl, xh, xl, work, theirs, leave,
-    acc, rl, rs, mbuf, dx, dh, dl, packed, ra1, rb1, ra2, rb2, share, rz, piece, gz,
+    graw, s_ref, ga, gb, g, ah, al, ph, plo, bh, bl, wh, wl, xh, xl, work, theirs, dall, dother,
+    acc, rl, rs, mbuf, dx, dh, dl, packed, ra1, rb1, half, rz, piece, gz,
     msem, gsem, ls, lr, ss, sr, als, alr, ass, asr, cs, cr,
-    a1s, a1r, b1s, b1r, a2s, a2r, b2s, b2r, z1s, z1r, z2s, z2r,
-    ga1s, ga1r, gb1s, gb1r, ga2s, ga2r, gb2s, gb2r, gcs, gcr, dsem, usem, ready,
+    a1s, a1r, b1s, b1r, ms, mr, z2s, z2r,
+    ga1s, ga1r, gb1s, gb1r, ga2s, ga2r, gb2s, gb2r, gcs, gcr, dsem, usem, ready, summed,
 ):
     z = lax.axis_index("dp")
     f = lax.axis_index("fsdp")
@@ -90,6 +90,7 @@
         return pl.ds(k * W, W)
 
     started = []
+    local = []
 
     def go(copy):
         copy.start()
@@ -141,6 +142,11 @@
         hops["u", 0, k] = go(gather_up(0, k))
         hops["d", 0, k] = go(gather_down(0, k))
 
+    pl.semaphore_wait(ready, len(beside))
+    around = [device((x + o) % 4, y, z, c) for o in (1, 2, 3)] + [device(x, (y + o) % 4, z, c) for o in (1, 2, 3)]
+    for target in around:
+        pl.semaphore_signal(summed, inc=1, device_id=target, device_id_type=MESH)
+
     for k in range(SUB):
         mine[k].wait_recv()
         d = dx[:, cols(k)]
@@ -173,111 +179,140 @@
     pa = (x * (1 - c) + y * c, y * (1 - c) + x * c)
     pb = (pa[1], pa[0])
 
-    def on_a(first, second):
-        return device(first * (1 - c) + second * c, second * (1 - c) + first * c, z, c)
-
-    def on_b(first, second):
-        return on_a(second, first)
+    def on_a(first, second, plane):
+        return device(first * (1 - c) + second * c, second * (1 - c) + first * c, plane, c)
+
+    def on_b(first, second, plane):
+        return on_a(second, first, plane)
 
     paths = (
-        (0, BA, pa, on_a, ra1, ra2, a1s, a1r, a2s, a2r, ga, ga1s, ga1r, ga2s, ga2r),
-        (SPLIT, BB, pb, on_b, rb1, rb2, b1s, b1r, b2s, b2r, gb, gb1s, gb1r, gb2s, gb2r),
+        (0, BA, pa, on_a, ra1, a1s, a1r, ga, ga1s, ga1r, ga2s, ga2r),
+        (SPLIT, BB, pb, on_b, rb1, b1s, b1r, gb, gb1s, gb1r, gb2s, gb2r),
     )
     order = (2, 1, 3)
 
     first_hops = []
 
-    def start_first(base, rows, at, on, r1, r2, s1, t1, *_):
+    def start_first(base, rows, at, on, r1, s1, t1, *_):
         size = 4 * rows
         for o in order:
             to = (at[0] + o) % 4
             src = packed.at[pl.ds(pl.multiple_of(base + to * size, 8), size)]
-            first_hops.append(go(remote(src, r1.at[o - 1], s1.at[o - 1], t1.at[o - 1], on(to, at[1]))))
-
-    pl.semaphore_wait(ready, len(beside))
+            first_hops.append(go(remote(src, r1.at[o - 1], s1.at[o - 1], t1.at[o - 1], on(to, at[1], z))))
+
     start_first(*paths[0])
     row_blocks(2)
     for b in range(2):
         packed[(9 + b) * 128 : (10 + b) * 128, :] = gram(2 * c + b, 2 * c + b + 3, 128)
     start_first(*paths[1])
 
+    def settle(offset):
+        at = chunk(offset)
+        nm_ref[at] = MOMENTUM_FACTOR * mbuf[at] + s_ref[at]
+        dall[at] = s_ref[at] + MOMENTUM_FACTOR * nm_ref[at]
+
+    settle(0)
     for k in range(SUB):
         hops["u", 0, k].wait_recv()
         hops["u", 1, k] = go(gather_up(1, k))
         hops["d", 0, k].wait_recv()
         hops["d", 1, k] = go(gather_down(1, k))
 
-    second_hops = []
-    for n, (base, rows, (p1, p2), on, r1, r2, s1, t1, s2, t2, *_) in enumerate(paths):
+    pl.semaphore_wait(summed, len(around))
+    for n, (base, rows, (p1, p2), on, r1, *_) in enumerate(paths):
         size = 4 * rows
         for hop in first_hops[3 * n : 3 * n + 3]:
             hop.wait_recv()
         own = pl.ds(pl.multiple_of(base + p1 * size, 8), size)
-        r1[3] = (packed[own, :] + r1[0]) + (r1[1] + r1[2])
-        for o in order:
+        total = (packed[own, :] + r1[0]) + (r1[1] + r1[2])
+        for i in range(4):
+            half[n, i, :rows] = total[i * rows : (i + 1) * rows]
+            if rows < 48:
+                half[n, i, rows:] = jnp.zeros((48 - rows, 128), F32)
+        for o in (2, 1, 3, 0):
             to = (p2 + o) % 4
-            src = r1.at[3, pl.ds(pl.multiple_of(to * rows, 8), rows)]
-            second_hops.append(go(remote(src, r2.at[o - 1], s2.at[o - 1], t2.at[o - 1], on(p1, to))))
-    for n, (base, rows, (p1, p2), on, r1, r2, *_) in enumerate(paths):
-        for hop in second_hops[3 * n : 3 * n + 3]:
-            hop.wait_recv()
-        own = pl.ds(pl.multiple_of(p2 * rows, 8), rows)
-        start = 0 if n == 0 else BA
-        share[start : start + rows, :] = (r1[3, own, :] + r2[0]) + (r2[1] + r2[2])
-    share[BA + BB : 96, :] = jnp.zeros((96 - BA - BB, 128), F32)
-
-    quarter = []
-    for o in (2, 1, 3):
-        to = (q + o) % 4
-        src = share.at[pl.ds(pl.multiple_of(to * 24, 8), 24)]
-        quarter.append(go(remote(src, rz.at[o - 1], z1s.at[o - 1], z1r.at[o - 1], device(x, y, layer * 4 + to, c))))
-    for hop in quarter:
-        hop.wait_recv()
+            for h in range(2):
+                plane = 2 * n + h
+                copy = remote(
+                    half.at[n, to, pl.ds(24 * h, 24)], rz.at[4 * o + q], ms.at[n, o, h], mr.at[o, q],
+                    on(p1, to, 4 * layer + plane),
+                )
+                if o > 0:
+                    go(copy)
+                else:
+                    pl.when(q != plane)(copy.start)
+                    local.append((q != plane, copy))
+    settle(1)
+    settle(-1)
+    mine_n, mine_h = q // 2, q % 2
+    mine_2 = pa[1] * (1 - mine_n) + pb[1] * mine_n
+    rz[q] = half[mine_n, mine_2, pl.ds(pl.multiple_of(24 * mine_h, 8), 24)]
+    for o in range(4):
+        for plane in range(4):
+            copy = remote(piece, rz.at[4 * o + plane], ms.at[0, 0, 0], mr.at[o, plane], other)
+            if o > 0:
+                copy.wait_recv()
+            else:
+                pl.when(q != plane)(copy.wait_recv)
+    sums = [rz[i] for i in range(16)]
+    while len(sums) > 1:
+        sums = [sums[2 * i] + sums[2 * i + 1] for i in range(len(sums) // 2)]
     at = pl.ds(pl.multiple_of(q * 24, 8), 24)
-    total = (share[at, :] + rz[0]) + (rz[1] + rz[2])
-    piece[...] = total
-    gz[layer, at, :] = total
+    piece[...] = sums[0]
+    gz[layer, at, :] = sums[0]
     for o in (4, 3, 5, 2, 6, 1, 7):
         go(remote(piece, gz.at[layer, at], z2s.at[o - 1], z2r.at[z], device(x, y, (z + o) % NZ, c)))
 
-    near, far = [], []
-
-    def start_gather(n, base, rows, at, on, r1, r2, s1, t1, s2, t2, out, u1, v1, u2, v2):
-        for plane in (2 * n, 2 * n + 1, 2 * n + 4, 2 * n + 5):
-
-            @pl.when(z != plane)
-            def _():
-                land = gz.at[plane // 4, pl.ds(plane % 4 * 24, 24)]
-                remote(piece, land, z2s.at[0], z2r.at[plane], other).wait_recv()
-
-        p1, p2 = at
-        start = 0 if n == 0 else BA
-        out[c, p1, p2] = gz[:, start : start + rows, :]
-        block = out.at[c, p1, p2]
+    layers = (layer, 1 - layer)
+    near, far = {}, {}
+
+    def start_far(t, n, j):
+        base, rows, (p1, p2), on, r1, s1, t1, out, u1, v1, u2, v2 = paths[n]
+        block = out.at[c, p1, (p2 + 4 - j) % 4, layers[t]]
         for o in order:
-            near.append(go(remote(block, block, u1.at[o - 1], v1.at[o - 1], on(p1, (p2 + o) % 4))))
-        for o in order:
-            far.append(go(remote(block, block, u2.at[o - 1, 0], v2.at[o - 1, 0], on((p1 + o) % 4, p2))))
-
-    for n in range(2):
-        start_gather(n, *paths[n])
+            far[t, n, o, j] = go(
+                remote(block, block, u2.at[t, o - 1, j], v2.at[t, o - 1, j], on((p1 + o) % 4, p2, z))
+            )
+
+    for t in range(2):
+        for n, (base, rows, (p1, p2), on, r1, s1, t1, out, u1, v1, u2, v2) in enumerate(paths):
+            for h in range(2):
+                plane = 4 * layers[t] + 2 * n + h
+                land = gz.at[layers[t], pl.ds(48 * n + 24 * h, 24)]
+                arrival = remote(piece, land, z2s.at[0], z2r.at[plane], other)
+                if t == 0:
+                    pl.when(z != plane)(arrival.wait_recv)
+                else:
+                    arrival.wait_recv()
+            out[c, p1, p2, layers[t]] = gz[layers[t], 48 * n : 48 * n + rows, :]
+            block = out.at[c, p1, p2, layers[t]]
+            for o in order:
+                near[t, n, o] = go(
+                    remote(block, block, u1.at[t, o - 1], v1.at[t, o - 1], on(p1, (p2 + o) % 4, z))
+                )
+            start_far(t, n, 0)
 
     for k in range(SUB):
         hops["u", 1, k].wait_recv()
         hops["u", 2, k] = go(gather_up(2, k))
         hops["d", 1, k].wait_recv()
         hops["d", 2, k] = go(gather_down(2, k))
-
-    for i, o in enumerate(order):
-        for n, (base, rows, (p1, p2), on, r1, r2, s1, t1, s2, t2, out, u1, v1, u2, v2) in enumerate(paths):
-            near[3 * n + i].wait_recv()
-            block = out.at[c, p1, (p2 + 4 - o) % 4]
-            for e in order:
-                far.append(go(remote(block, block, u2.at[e - 1, o], v2.at[e - 1, o], on((p1 + e) % 4, p2))))
+    settle(2)
+    settle(-2)
+
+    for t in range(2):
+        for o in order:
+            for n in range(2):
+                near[t, n, o].wait_recv()
+                start_far(t, n, o)
 
     for k in range(SUB):
         hops["u", 2, k].wait_recv()
         hops["u", 3, k] = go(gather_up(3, k))
+    for k in range(SUB):
+        hops["d", 2, k].wait_recv()
+    settle(-3)
+    settle(3)
 
     crossing = []
 
@@ -288,12 +323,16 @@
 
     for n in range(2):
         cross(n, paths[n][2][0], 0)
-    for i, o in enumerate(order):
+    for o in order:
         for n in range(2):
-            far[3 * n + i].wait_recv()
-            for j in range(3):
-                far[6 + 6 * j + 3 * n + i].wait_recv()
+            for t in range(2):
+                for j in range(4):
+                    far[t, n, o, j].wait_recv()
             cross(n, (paths[n][2][0] + 4 - o) % 4, o)
+    for k in range(SUB):
+        hops["u", 3, k].wait_recv()
+    settle(-4)
+    handed = go(remote(dall.at[pl.ds(4 * (1 - c), 4)], dother, dsem.at[0], dsem.at[1], other))
     for hop in crossing:
         hop.wait_recv()
 
@@ -331,19 +370,6 @@
 
     symmetric_product((ah, al), (ah, al), (ph, plo), polynomial)
 
-    for k in range(SUB):
-        hops["d", 2, k].wait_recv()
-        hops["u", 3, k].wait_recv()
-    for i in range(NZ):
-        nm_ref[i] = MOMENTUM_FACTOR * mbuf[i] + s_ref[i]
-    for i in range(4):
-        at = 4 * (1 - c) + i
-        leave[i * CH : (i + 1) * CH, :] = s_ref[at] + MOMENTUM_FACTOR * nm_ref[at]
-    handed = go(remote(leave, work.at[pl.ds(224, 224)], dsem.at[0], dsem.at[1], other))
-    for i in range(4):
-        at = 4 * c + i
-        work[i * CH : (i + 1) * CH, :] = s_ref[at] + MOMENTUM_FACTOR * nm_ref[at]
-
     symmetric_product((ph, plo), (ah, al), (bh, bl))
     symmetric_product((ph, plo), (bh, bl), (ah, al))
 
@@ -351,8 +377,8 @@
     factor = UPDATE_FACTOR * math.sqrt(max(D, R))
     halves = (slice(224, 448), slice(0, 224))
     every = slice(0, R)
-    for rows in halves:
-        put(wh, wl, rows, every, work[rows, :])
+    put(wh, wl, halves[1], every, dall[pl.ds(4 * c, 4)].reshape(224, R))
+    put(wh, wl, halves[0], every, dother[...].reshape(224, R))
     for rows in halves:
         x1 = dot3((wh[rows, :], wl[rows, :]), (ph[...], plo[...])) * scale
         work[rows, :] = QUINTIC_LINEAR * x1
@@ -371,6 +397,8 @@
     back.wait_recv()
     for copy in started:
         copy.wait_send()
+    for condition, copy in local:
+        pl.when(condition)(copy.wait_send)
 
 
 def dot3(left, right):
@@ -444,7 +472,8 @@
             pltpu.VMEM((R, R), F32), half, half, half, half, half, half, rows, rows, rows, rows,
             pltpu.VMEM((NZ * CH, R), F32),
             pltpu.VMEM((224, R), F32),
-            pltpu.VMEM((224, R), F32),
+            pltpu.VMEM((NZ, CH, R), F32),
+            pltpu.VMEM((4, CH, R), F32),
             pltpu.VMEM((NZ, CH, R), F32),
             pltpu.VMEM((4, CH, R), F32),
             pltpu.VMEM((3, CH, R), F32),
@@ -453,12 +482,10 @@
             pltpu.VMEM((2 * CH, R + W), BF16),
             pltpu.VMEM((2 * CH, R + W), BF16),
             pltpu.VMEM((BLOCKS * 128, 128), F32),
-            pltpu.VMEM((4, 4 * BA, 128), F32),
-            pltpu.VMEM((4, 4 * BB, 128), F32),
-            pltpu.VMEM((3, BA, 128), F32),
-            pltpu.VMEM((3, BB, 128), F32),
-            pltpu.VMEM((96, 128), F32),
-            pltpu.VMEM((3, 24, 128), F32),
+            pltpu.VMEM((3, 4 * BA, 128), F32),
+            pltpu.VMEM((3, 4 * BB, 128), F32),
+            pltpu.VMEM((2, 4, 48, 128), F32),
+            pltpu.VMEM((16, 24, 128), F32),
             pltpu.VMEM((24, 128), F32),
             pltpu.VMEM((2, 96, 128), F32),
             sem,
@@ -466,13 +493,14 @@
         ]
         + [sem((4, SUB)), sem((4, SUB)), sem((3, SUB)), sem((3, SUB))] * 2
         + [sem((SUB,))] * 2
-        + [sem((3,))] * 10
+        + [sem((3,))] * 4
+        + [sem((2, 4, 2)), sem((4, 4))]
         + [sem((8,))] * 2
-        + [sem((3,))] * 4
-        + [sem((3, 4))] * 4
+        + [sem((2, 3))] * 4
+        + [sem((2, 3, 4))] * 4
         + [sem((2, 4))] * 2
         + [sem((2,))] * 2
-        + [pltpu.SemaphoreType.REGULAR],
+        + [pltpu.SemaphoreType.REGULAR] * 2,
         compiler_params=pltpu.CompilerParams(collective_id=0, has_side_effects=True, vmem_limit_bytes=34 << 20),
         name="gram",
     )(grads, momentum)

time: 79.4 us -> 76.8 us (0.967)
  Pallas kernels: 78.7 us -> 76 us
    pallas_call x1, Pallas kernels: 76.7 us -> 74 us  [shards(): pl.pallas_call(gram_kernel, out_shape=(jax.ShapeDtypeStruct((NZ, CH, R),...]
where the time goes in v4:
time: 76.8 us; the launch traced here: 76.7 us
  Pallas kernels  76 us (99%)
    pallas_call x1, Pallas kernels, shards(): pl.pallas_call(gram_kernel, out_shape=(jax.ShapeDtypeStruct((NZ, CH, R),...  74 us
    pallas_call x1, Pallas kernels, shards(): pl.pallas_call(update_kernel, out_shape=(like, like, like), in_specs=[vme...  2.03 us

profile of v4, /device:TPU:1, one launch (start us, length us, event | category | flops | bytes accessed | tf_op | source)
XLA Modules:
  0.0 76.7 jit_solution(3868384191230177428)
XLA Ops:
  0.6 0.0 copy-start
  0.6 74.0 %gram.1 = (f32[8,56,768]{2,1,0:T(8,128)S(1)}, f32[2,224,768]{2,1,0:T(8,128)S(1)}) custom-call(bf16[448,768]{1,0:T(8,128)(2,1)} %bitcast.12, f32[8,56,768]{2,1,0:T(8,128)} %bitcast.11), custom_call_target="tpu_custom_call" | custom-call | tf_op jit(solution)/shard_map/gram/pallas_call | solution.py:459
  74.6 0.0 copy-done
  74.6 2.0 %update.1 = (f32[448,768]{1,0:T(8,128)}, f32[448,768]{1,0:T(8,128)}, f32[448,768]{1,0:T(8,128)}) custom-call(f32[448,768]{1,0:T(8,128)S(1)} %bitcast.9, f32[448,768]{1,0:T(8,128)S(1)} %bitcast.10, f32[448,768]{1,0:T(8,128)S(1)} %bitcast.8), custom_call_target="tpu_custom_call" | custom-call | tf_op jit(solution)/shard_map/update/pallas_call | solution.py:508
Async XLA Ops:
  0.6 74.0 %copy-start = (f32[2,224,768]{2,1,0:T(8,128)S(1)}, f32[2,224,768]{2,1,0:T(8,128)}, u32[]{:S(2)}) copy-start(f32[2,224,768]{2,1,0:T(8,128)} %param.5) | copy-start | bytes 4128772

commit v5 on v4

--- a/solution.py
+++ b/solution.py
@@ -27,8 +27,8 @@
 CH = 56
 SUB = 3
 W = R // SUB
-BA, BB = 48, 40
-BLOCKS = 11
+BA, BB = 40, 32
+BLOCKS = 9
 SPLIT = 16 * BA
 
 
@@ -45,10 +45,10 @@
 def gram_kernel(
     g_ref, m_ref, nm_ref, up_ref,
     graw, s_ref, ga, gb, g, ah, al, ph, plo, bh, bl, wh, wl, xh, xl, work, theirs, dall, dother,
-    acc, rl, rs, mbuf, dx, dh, dl, packed, ra1, rb1, half, rz, piece, gz,
+    acc, rl, rs, mbuf, dx, dh, dl, packed, tile, rt, ra1, rb1, half, rz, piece, gz,
     msem, gsem, ls, lr, ss, sr, als, alr, ass, asr, cs, cr,
-    a1s, a1r, b1s, b1r, ms, mr, z2s, z2r,
-    ga1s, ga1r, gb1s, gb1r, ga2s, ga2r, gb2s, gb2r, gcs, gcr, dsem, usem, ready, summed,
+    a1s, a1r, b1s, b1r, ts, tr, ms, mr, z2s, z2r,
+    ga1s, ga1r, gb1s, gb1r, ga2s, ga2r, gb2s, gb2r, dsem, usem, ready, summed,
 ):
     z = lax.axis_index("dp")
     f = lax.axis_index("fsdp")
@@ -158,6 +158,9 @@
             dh[:, R : R + W] = hi
             dl[:, R : R + W] = lo
 
+    ROW = lax.broadcasted_iota(jnp.int32, (128, 128), 0)
+    COL = lax.broadcasted_iota(jnp.int32, (128, 128), 1)
+
     def gram(first, second, width):
         li = pl.ds(pl.multiple_of(first * 128, 128), 128)
         ri = pl.ds(pl.multiple_of(second * 128, 128), width)
@@ -168,13 +171,22 @@
         lh, ll, rh, rlo = dh[:, li], dl[:, li], dh[:, ri], dl[:, ri]
         return dot(lh, rh) + (dot(lh, rlo) + dot(ll, rh))
 
-    def row_blocks(a):
-        block = gram(3 * c + a, 3 * c + a, 384)
-        for k in range(3):
-            packed[(3 * a + k) * 128 : (3 * a + k + 1) * 128, :] = block[:, k * 128 : (k + 1) * 128]
-
-    row_blocks(0)
-    row_blocks(1)
+    for a in range(3):
+        block = gram(3 * c + a, 3 * c + a + 1, 256)
+        packed[2 * a * 128 : (2 * a + 1) * 128, :] = block[:, :128]
+        packed[(2 * a + 1) * 128 : (2 * a + 2) * 128, :] = block[:, 128:]
+
+    def corner_blocks():
+        @pl.when(c == 0)
+        def _():
+            for e in range(3):
+                packed[(6 + e) * 128 : (7 + e) * 128, :] = gram(e, e + 3, 128)
+
+        @pl.when(c == 1)
+        def _():
+            upper = ROW <= COL
+            for e in range(3):
+                packed[(6 + e) * 128 : (7 + e) * 128, :] = jnp.where(upper, gram(e, e, 128), gram(e + 3, e + 3, 128))
 
     pa = (x * (1 - c) + y * c, y * (1 - c) + x * c)
     pb = (pa[1], pa[0])
@@ -201,10 +213,13 @@
             first_hops.append(go(remote(src, r1.at[o - 1], s1.at[o - 1], t1.at[o - 1], on(to, at[1], z))))
 
     start_first(*paths[0])
-    row_blocks(2)
-    for b in range(2):
-        packed[(9 + b) * 128 : (10 + b) * 128, :] = gram(2 * c + b, 2 * c + b + 3, 128)
+    corner_blocks()
     start_first(*paths[1])
+    tile[...] = jnp.zeros((8, 128), F32)
+    for e in range(3):
+        d = dx[:, (e + 3) * 128 : (e + 4) * 128]
+        tile[e : e + 1, :] = jnp.sum(d * d, axis=0, keepdims=True)
+    tiles = [go(remote(tile, rt.at[o - 1], ts.at[o - 1], tr.at[o - 1], on_a((pa[0] + o) % 4, pa[1], z))) for o in order]
 
     def settle(offset):
         at = chunk(offset)
@@ -225,10 +240,19 @@
             hop.wait_recv()
         own = pl.ds(pl.multiple_of(base + p1 * size, 8), size)
         total = (packed[own, :] + r1[0]) + (r1[1] + r1[2])
+        if n == 0:
+            for hop in tiles:
+                hop.wait_recv()
+            squares = (tile[...] + rt[0]) + (rt[1] + rt[2])
         for i in range(4):
-            half[n, i, :rows] = total[i * rows : (i + 1) * rows]
-            if rows < 48:
-                half[n, i, rows:] = jnp.zeros((48 - rows, 128), F32)
+            if n == 0:
+                half[0, i, :BA] = total[i * BA : (i + 1) * BA]
+                half[0, i, BA:] = squares
+            else:
+                half[1, i, 0:16] = total[i * BB : i * BB + 16]
+                half[1, i, 16:24] = squares
+                half[1, i, 24:40] = total[i * BB + 16 : (i + 1) * BB]
+                half[1, i, 40:48] = squares
         for o in (2, 1, 3, 0):
             to = (p2 + o) % 4
             for h in range(2):
@@ -259,38 +283,40 @@
         sums = [sums[2 * i] + sums[2 * i + 1] for i in range(len(sums) // 2)]
     at = pl.ds(pl.multiple_of(q * 24, 8), 24)
     piece[...] = sums[0]
-    gz[layer, at, :] = sums[0]
     for o in (4, 3, 5, 2, 6, 1, 7):
-        go(remote(piece, gz.at[layer, at], z2s.at[o - 1], z2r.at[z], device(x, y, (z + o) % NZ, c)))
-
-    layers = (layer, 1 - layer)
+        go(remote(piece, gz.at[c, at], z2s.at[o], z2r.at[c, q], device(x, y, (z + o) % NZ, layer)))
+
+    @pl.when(layer == c)
+    def _():
+        gz[c, at, :] = piece[...]
+
+    copy = remote(piece, gz.at[c, at], z2s.at[0], z2r.at[c, q], other)
+    pl.when(layer != c)(copy.start)
+    local.append((layer != c, copy))
+
     near, far = {}, {}
 
-    def start_far(t, n, j):
+    def start_far(n, j):
         base, rows, (p1, p2), on, r1, s1, t1, out, u1, v1, u2, v2 = paths[n]
-        block = out.at[c, p1, (p2 + 4 - j) % 4, layers[t]]
+        block = out.at[p1, (p2 + 4 - j) % 4]
         for o in order:
-            far[t, n, o, j] = go(
-                remote(block, block, u2.at[t, o - 1, j], v2.at[t, o - 1, j], on((p1 + o) % 4, p2, z))
-            )
-
-    for t in range(2):
-        for n, (base, rows, (p1, p2), on, r1, s1, t1, out, u1, v1, u2, v2) in enumerate(paths):
+            far[n, o, j] = go(remote(block, block, u2.at[o - 1, j], v2.at[o - 1, j], on((p1 + o) % 4, p2, z)))
+
+    for n, (base, rows, (p1, p2), on, r1, s1, t1, out, u1, v1, u2, v2) in enumerate(paths):
+        for quarter in (2 * n, 2 * n + 1):
             for h in range(2):
-                plane = 4 * layers[t] + 2 * n + h
-                land = gz.at[layers[t], pl.ds(48 * n + 24 * h, 24)]
-                arrival = remote(piece, land, z2s.at[0], z2r.at[plane], other)
-                if t == 0:
-                    pl.when(z != plane)(arrival.wait_recv)
-                else:
-                    arrival.wait_recv()
-            out[c, p1, p2, layers[t]] = gz[layers[t], 48 * n : 48 * n + rows, :]
-            block = out.at[c, p1, p2, layers[t]]
-            for o in order:
-                near[t, n, o] = go(
-                    remote(block, block, u1.at[t, o - 1], v1.at[t, o - 1], on(p1, (p2 + o) % 4, z))
-                )
-            start_far(t, n, 0)
+                arrival = remote(piece, gz.at[h, pl.ds(24 * quarter, 24)], z2s.at[0], z2r.at[h, quarter], other)
+                pl.when((layer != c) | (c != h) | (q != quarter))(arrival.wait_recv)
+        if n == 0:
+            out[p1, p2] = gz[:, 0:BA, :]
+        else:
+            out[p1, p2, :, 0:16] = gz[:, 48:64, :]
+            out[p1, p2, :, 16:32] = gz[:, 72:88, :]
+        block = out.at[p1, p2]
+        for o in order:
+            near[n, o] = go(remote(block, block, u1.at[o - 1], v1.at[o - 1], on(p1, (p2 + o) % 4, z)))
+    for n in range(2):
+        start_far(n, 0)
 
     for k in range(SUB):
         hops["u", 1, k].wait_recv()
@@ -300,11 +326,10 @@
     settle(2)
     settle(-2)
 
-    for t in range(2):
-        for o in order:
-            for n in range(2):
-                near[t, n, o].wait_recv()
-                start_far(t, n, o)
+    for o in order:
+        for n in range(2):
+            near[n, o].wait_recv()
+            start_far(n, o)
 
     for k in range(SUB):
         hops["u", 2, k].wait_recv()
@@ -314,48 +339,40 @@
     settle(-3)
     settle(3)
 
-    crossing = []
-
-    def cross(n, first, o):
-        out = (ga, gb)[n]
-        block = out.at[c, first, :, 1 - c]
-        crossing.append(go(remote(block, block, gcs.at[n, o], gcr.at[n, o], other)))
-
-    for n in range(2):
-        cross(n, paths[n][2][0], 0)
-    for o in order:
-        for n in range(2):
-            for t in range(2):
-                for j in range(4):
-                    far[t, n, o, j].wait_recv()
-            cross(n, (paths[n][2][0] + 4 - o) % 4, o)
     for k in range(SUB):
         hops["u", 3, k].wait_recv()
     settle(-4)
     handed = go(remote(dall.at[pl.ds(4 * (1 - c), 4)], dother, dsem.at[0], dsem.at[1], other))
-    for hop in crossing:
+    for hop in far.values():
         hop.wait_recv()
 
-    trace = jnp.zeros((), F32)
-    eye = lax.broadcasted_iota(jnp.int32, (128, 128), 0) == lax.broadcasted_iota(jnp.int32, (128, 128), 1)
+    diagonals = gz[0, BA : BA + 8, :]
+    trace = jnp.sum(diagonals)
+
+    def place(i, j, block):
+        g[i * 128 : (i + 1) * 128, j * 128 : (j + 1) * 128] = block
+
     for h in range(2):
-        rows_a = ga[h, :, :, c].reshape(16 * BA, 128)
-        rows_b = gb[h, :, :, c].reshape(16 * BB, 128)
+        turned = h + c - 2 * h * c
+        places = [(i * (1 - turned) + j * turned, j * (1 - turned) + i * turned) for i in range(4) for j in range(4)]
+        rows_a = jnp.concatenate([ga[i, j, h] for i, j in places], axis=0)
+        rows_b = jnp.concatenate([gb[i, j, h] for i, j in places], axis=0)
         for b in range(BLOCKS):
-            if b < 9:
-                i = 3 * h + b // 3
-                j = (i + b % 3) % 6
+            block = rows_a[b * 128 : (b + 1) * 128] if b < 5 else rows_b[(b - 5) * 128 : (b - 4) * 128]
+            if b < 6:
+                i = 3 * h + b // 2
+                j = (i + 1 + b % 2) % 6
             else:
-                i = 2 * h + b - 9
-                j = (i + 3) % 6
-            if i == 3 and j == 0:
-                continue
-            block = rows_a[b * 128 : (b + 1) * 128] if b < 6 else rows_b[(b - 6) * 128 : (b - 5) * 128]
-            g[i * 128 : (i + 1) * 128, j * 128 : (j + 1) * 128] = block
-            if i == j:
-                trace = trace + jnp.sum(jnp.where(eye, block, 0.0))
+                i, j = b - 6, b - 3
+            if b < 6 or h == 0:
+                place(i, j, block)
+                place(j, i, block.T)
             else:
-                g[j * 128 : (j + 1) * 128, i * 128 : (i + 1) * 128] = block.T
+                trace = trace + jnp.sum(jnp.where(ROW == COL, block, 0.0))
+                above = jnp.where(ROW < COL, block, 0.0)
+                below = jnp.where(ROW > COL, block, 0.0)
+                place(i, i, jnp.where(ROW <= COL, block, 0.0) + above.T)
+                place(j, j, below + below.T + jnp.where(ROW == COL, diagonals[i : i + 1, :], 0.0))
     inverse = 1.0 / (jnp.sqrt(jnp.broadcast_to(trace, (8, 128))) + NORM_EPSILON)
     scale = inverse[0:1, 0:1]
     square = scale * scale
@@ -467,8 +484,8 @@
         scratch_shapes=[
             pltpu.VMEM((NZ * CH, R), BF16),
             pltpu.VMEM((NZ, CH, R), F32),
-            pltpu.VMEM((2, 4, 4, 2, BA, 128), F32),
-            pltpu.VMEM((2, 4, 4, 2, BB, 128), F32),
+            pltpu.VMEM((4, 4, 2, BA, 128), F32),
+            pltpu.VMEM((4, 4, 2, BB, 128), F32),
             pltpu.VMEM((R, R), F32), half, half, half, half, half, half, rows, rows, rows, rows,
             pltpu.VMEM((NZ * CH, R), F32),
             pltpu.VMEM((224, R), F32),
@@ -482,6 +499,8 @@
             pltpu.VMEM((2 * CH, R + W), BF16),
             pltpu.VMEM((2 * CH, R + W), BF16),
             pltpu.VMEM((BLOCKS * 128, 128), F32),
+            pltpu.VMEM((8, 128), F32),
+            pltpu.VMEM((3, 8, 128), F32),
             pltpu.VMEM((3, 4 * BA, 128), F32),
             pltpu.VMEM((3, 4 * BB, 128), F32),
             pltpu.VMEM((2, 4, 48, 128), F32),
@@ -493,12 +512,11 @@
         ]
         + [sem((4, SUB)), sem((4, SUB)), sem((3, SUB)), sem((3, SUB))] * 2
         + [sem((SUB,))] * 2
+        + [sem((3,))] * 6
+        + [sem((2, 4, 2)), sem((4, 4))]
+        + [sem((8,)), sem((2, 4))]
         + [sem((3,))] * 4
-        + [sem((2, 4, 2)), sem((4, 4))]
-        + [sem((8,))] * 2
-        + [sem((2, 3))] * 4
-        + [sem((2, 3, 4))] * 4
-        + [sem((2, 4))] * 2
+        + [sem((3, 4))] * 4
         + [sem((2,))] * 2
         + [pltpu.SemaphoreType.REGULAR] * 2,
         compiler_params=pltpu.CompilerParams(collective_id=0, has_side_effects=True, vmem_limit_bytes=34 << 20),

time: 76.8 us -> 74.1 us (0.965)
  Pallas kernels: 76 us -> 73.4 us
    pallas_call x1, Pallas kernels: 74 us -> 71.3 us  [shards(): pl.pallas_call(gram_kernel, out_shape=(jax.ShapeDtypeStruct((NZ, CH, R),...]
where the time goes in v5:
time: 74.1 us; the launch traced here: 74 us
  Pallas kernels  73.4 us (99%)
    pallas_call x1, Pallas kernels, shards(): pl.pallas_call(gram_kernel, out_shape=(jax.ShapeDtypeStruct((NZ, CH, R),...  71.3 us
    pallas_call x1, Pallas kernels, shards(): pl.pallas_call(update_kernel, out_shape=(like, like, like), in_specs=[vme...  2.03 us

profile of v5, /device:TPU:1, one launch (start us, length us, event | category | flops | bytes accessed | tf_op | source)
XLA Modules:
  0.0 74.0 jit_solution(5900575833769933485)
XLA Ops:
  0.6 0.0 copy-start
  0.6 71.3 %gram.1 = (f32[8,56,768]{2,1,0:T(8,128)S(1)}, f32[2,224,768]{2,1,0:T(8,128)S(1)}) custom-call(bf16[448,768]{1,0:T(8,128)(2,1)} %bitcast.12, f32[8,56,768]{2,1,0:T(8,128)} %bitcast.11), custom_call_target="tpu_custom_call" | custom-call | tf_op jit(solution)/shard_map/gram/pallas_call | solution.py:476
  72.0 0.0 copy-done
  72.0 2.0 %update.1 = (f32[448,768]{1,0:T(8,128)}, f32[448,768]{1,0:T(8,128)}, f32[448,768]{1,0:T(8,128)}) custom-call(f32[448,768]{1,0:T(8,128)S(1)} %bitcast.9, f32[448,768]{1,0:T(8,128)S(1)} %bitcast.10, f32[448,768]{1,0:T(8,128)S(1)} %bitcast.8), custom_call_target="tpu_custom_call" | custom-call | tf_op jit(solution)/shard_map/update/pallas_call | solution.py:526
Async XLA Ops:
  0.6 71.4 %copy-start = (f32[2,224,768]{2,1,0:T(8,128)S(1)}, f32[2,224,768]{2,1,0:T(8,128)}, u32[]{:S(2)}) copy-start(f32[2,224,768]{2,1,0:T(8,128)} %param.5) | copy-start | bytes 4128772

commit v6 on v5

--- a/solution.py
+++ b/solution.py
@@ -97,6 +97,14 @@
         started.append(copy)
         return copy
 
+    def drain():
+        for copy in started:
+            copy.wait_send()
+        for condition, copy in local:
+            pl.when(condition)(copy.wait_send)
+        started.clear()
+        local.clear()
+
     def long_hop(step, k):
         return remote(acc.at[chunk(4 - step), :, cols(k)], rl.at[step, :, cols(k)], ls.at[step, k], lr.at[step, k], up)
 
@@ -119,13 +127,13 @@
                 acc[at, :, cols(k)] = acc[at, :, cols(k)] + rs[step - 1, :, cols(k)]
                 hops["s", step, k] = go(short_hop(step, k))
 
-    def gather_up(step, k):
-        at = chunk(-step)
-        return remote(s_ref.at[at, :, cols(k)], s_ref.at[at, :, cols(k)], als.at[step, k], alr.at[step, k], up)
-
-    def gather_down(step, k):
-        at = chunk(step)
-        return remote(s_ref.at[at, :, cols(k)], s_ref.at[at, :, cols(k)], ass.at[step, k], asr.at[step, k], down)
+    def gather_up(step):
+        block = s_ref.at[chunk(-step)]
+        hops["u", step] = go(remote(block, block, als.at[step], alr.at[step], up))
+
+    def gather_down(step):
+        block = s_ref.at[chunk(step)]
+        hops["d", step] = go(remote(block, block, ass.at[step], asr.at[step], down))
 
     fetch.wait()
     mine = []
@@ -139,8 +147,8 @@
         mine.append(
             go(remote(dx.at[pl.ds(0, CH), cols(k)], dx.at[pl.ds(CH, CH), cols(k)], cs.at[k], cr.at[k], other))
         )
-        hops["u", 0, k] = go(gather_up(0, k))
-        hops["d", 0, k] = go(gather_down(0, k))
+    gather_up(0)
+    gather_down(0)
 
     pl.semaphore_wait(ready, len(beside))
     around = [device((x + o) % 4, y, z, c) for o in (1, 2, 3)] + [device(x, (y + o) % 4, z, c) for o in (1, 2, 3)]
@@ -227,11 +235,10 @@
         dall[at] = s_ref[at] + MOMENTUM_FACTOR * nm_ref[at]
 
     settle(0)
-    for k in range(SUB):
-        hops["u", 0, k].wait_recv()
-        hops["u", 1, k] = go(gather_up(1, k))
-        hops["d", 0, k].wait_recv()
-        hops["d", 1, k] = go(gather_down(1, k))
+    hops["u", 0].wait_recv()
+    gather_up(1)
+    hops["d", 0].wait_recv()
+    gather_down(1)
 
     pl.semaphore_wait(summed, len(around))
     for n, (base, rows, (p1, p2), on, r1, *_) in enumerate(paths):
@@ -302,6 +309,7 @@
         for o in order:
             far[n, o, j] = go(remote(block, block, u2.at[o - 1, j], v2.at[o - 1, j], on((p1 + o) % 4, p2, z)))
 
+    gathering = len(started)
     for n, (base, rows, (p1, p2), on, r1, s1, t1, out, u1, v1, u2, v2) in enumerate(paths):
         for quarter in (2 * n, 2 * n + 1):
             for h in range(2):
@@ -317,30 +325,29 @@
             near[n, o] = go(remote(block, block, u1.at[o - 1], v1.at[o - 1], on(p1, (p2 + o) % 4, z)))
     for n in range(2):
         start_far(n, 0)
-
-    for k in range(SUB):
-        hops["u", 1, k].wait_recv()
-        hops["u", 2, k] = go(gather_up(2, k))
-        hops["d", 1, k].wait_recv()
-        hops["d", 2, k] = go(gather_down(2, k))
+    sent, started[:] = started[:gathering], started[gathering:]
+
+    hops["u", 1].wait_recv()
+    gather_up(2)
+    hops["d", 1].wait_recv()
+    gather_down(2)
     settle(2)
     settle(-2)
 
+    for copy in sent:
+        copy.wait_send()
     for o in order:
         for n in range(2):
             near[n, o].wait_recv()
             start_far(n, o)
 
-    for k in range(SUB):
-        hops["u", 2, k].wait_recv()
-        hops["u", 3, k] = go(gather_up(3, k))
-    for k in range(SUB):
-        hops["d", 2, k].wait_recv()
+    hops["u", 2].wait_recv()
+    gather_up(3)
+    hops["d", 2].wait_recv()
     settle(-3)
     settle(3)
 
-    for k in range(SUB):
-        hops["u", 3, k].wait_recv()
+    hops["u", 3].wait_recv()
     settle(-4)
     handed = go(remote(dall.at[pl.ds(4 * (1 - c), 4)], dother, dsem.at[0], dsem.at[1], other))
     for hop in far.values():
@@ -411,11 +418,8 @@
     theirs[...] = finish(halves[0])
     back = go(remote(theirs, up_ref.at[c], usem.at[0], usem.at[1], other))
     up_ref[c] = finish(halves[1])
+    drain()
     back.wait_recv()
-    for copy in started:
-        copy.wait_send()
-    for condition, copy in local:
-        pl.when(condition)(copy.wait_send)
 
 
 def dot3(left, right):
@@ -510,7 +514,8 @@
             sem,
             sem,
         ]
-        + [sem((4, SUB)), sem((4, SUB)), sem((3, SUB)), sem((3, SUB))] * 2
+        + [sem((4, SUB)), sem((4, SUB)), sem((3, SUB)), sem((3, SUB))]
+        + [sem((4,)), sem((4,)), sem((3,)), sem((3,))]
         + [sem((SUB,))] * 2
         + [sem((3,))] * 6
         + [sem((2, 4, 2)), sem((4, 4))]

time: 74.1 us -> 73.9 us (level)
  no operation moved by 1% of the time
where the time goes in v6:
time: 73.9 us; the launch traced here: 73.8 us
  Pallas kernels  73.2 us (99%)
    pallas_call x1, Pallas kernels, shards(): pl.pallas_call(gram_kernel, out_shape=(jax.ShapeDtypeStruct((NZ, CH, R),...  71.1 us
    pallas_call x1, Pallas kernels, shards(): pl.pallas_call(update_kernel, out_shape=(like, like, like), in_specs=[vme...  2.03 us

profile of v6, /device:TPU:1, one launch (start us, length us, event | category | flops | bytes accessed | tf_op | source)
XLA Modules:
  0.0 73.8 jit_solution(15249779346812099280)
XLA Ops:
  0.6 0.0 copy-start
  0.6 71.1 %gram.1 = (f32[8,56,768]{2,1,0:T(8,128)S(1)}, f32[2,224,768]{2,1,0:T(8,128)S(1)}) custom-call(bf16[448,768]{1,0:T(8,128)(2,1)} %bitcast.12, f32[8,56,768]{2,1,0:T(8,128)} %bitcast.11), custom_call_target="tpu_custom_call" | custom-call | tf_op jit(solution)/shard_map/gram/pallas_call | solution.py:480
  71.8 0.0 copy-done
  71.8 2.0 %update.1 = (f32[448,768]{1,0:T(8,128)}, f32[448,768]{1,0:T(8,128)}, f32[448,768]{1,0:T(8,128)}) custom-call(f32[448,768]{1,0:T(8,128)S(1)} %bitcast.9, f32[448,768]{1,0:T(8,128)S(1)} %bitcast.10, f32[448,768]{1,0:T(8,128)S(1)} %bitcast.8), custom_call_target="tpu_custom_call" | custom-call | tf_op jit(solution)/shard_map/update/pallas_call | solution.py:531
Async XLA Ops:
  0.6 71.2 %copy-start = (f32[2,224,768]{2,1,0:T(8,128)S(1)}, f32[2,224,768]{2,1,0:T(8,128)}, u32[]{:S(2)}) copy-start(f32[2,224,768]{2,1,0:T(8,128)} %param.5) | copy-start | bytes 4128772

commit v7 on v6

--- a/solution.py
+++ b/solution.py
@@ -306,8 +306,15 @@
     def start_far(n, j):
         base, rows, (p1, p2), on, r1, s1, t1, out, u1, v1, u2, v2 = paths[n]
         block = out.at[p1, (p2 + 4 - j) % 4]
-        for o in order:
+        for o in (1, 3) if j == 0 else order:
             far[n, o, j] = go(remote(block, block, u2.at[o - 1, j], v2.at[o - 1, j], on((p1 + o) % 4, p2, z)))
+
+    def pass_on(n):
+        base, rows, (p1, p2), on, r1, s1, t1, out, u1, v1, u2, v2 = paths[n]
+        source = (3, 1)[n]
+        far[n, source, 0].wait_recv()
+        block = out.at[(p1 + 4 - source) % 4, p2]
+        far[n, 2, 0] = go(remote(block, block, u2.at[1, 0], v2.at[1, 0], on((p1 + source) % 4, p2, z)))
 
     gathering = len(started)
     for n, (base, rows, (p1, p2), on, r1, s1, t1, out, u1, v1, u2, v2) in enumerate(paths):
@@ -340,6 +347,8 @@
         for n in range(2):
             near[n, o].wait_recv()
             start_far(n, o)
+    for n in range(2):
+        pass_on(n)
 
     hops["u", 2].wait_recv()
     gather_up(3)
@@ -350,8 +359,9 @@
     hops["u", 3].wait_recv()
     settle(-4)
     handed = go(remote(dall.at[pl.ds(4 * (1 - c), 4)], dother, dsem.at[0], dsem.at[1], other))
-    for hop in far.values():
-        hop.wait_recv()
+    for (n, o, j), hop in far.items():
+        if j != 0 or o != (3, 1)[n]:
+            hop.wait_recv()
 
     diagonals = gz[0, BA : BA + 8, :]
     trace = jnp.sum(diagonals)

time: 73.9 us -> 74.2 us (level)
  no operation moved by 1% of the time
where the time goes in v7:
time: 74.2 us; the launch traced here: 74.1 us
  Pallas kernels  73.5 us (99%)
    pallas_call x1, Pallas kernels, shards(): pl.pallas_call(gram_kernel, out_shape=(jax.ShapeDtypeStruct((NZ, CH, R),...  71.5 us
    pallas_call x1, Pallas kernels, shards(): pl.pallas_call(update_kernel, out_shape=(like, like, like), in_specs=[vme...  2.03 us

profile of v7, /device:TPU:1, one launch (start us, length us, event | category | flops | bytes accessed | tf_op | source)
XLA Modules:
  0.0 74.1 jit_solution(2143662974065244051)
XLA Ops:
  0.6 0.0 copy-start
  0.6 71.5 %gram.1 = (f32[8,56,768]{2,1,0:T(8,128)S(1)}, f32[2,224,768]{2,1,0:T(8,128)S(1)}) custom-call(bf16[448,768]{1,0:T(8,128)(2,1)} %bitcast.12, f32[8,56,768]{2,1,0:T(8,128)} %bitcast.11), custom_call_target="tpu_custom_call" | custom-call | tf_op jit(solution)/shard_map/gram/pallas_call | solution.py:490
  72.1 0.0 copy-done
  72.1 2.0 %update.1 = (f32[448,768]{1,0:T(8,128)}, f32[448,768]{1,0:T(8,128)}, f32[448,768]{1,0:T(8,128)}) custom-call(f32[448,768]{1,0:T(8,128)S(1)} %bitcast.9, f32[448,768]{1,0:T(8,128)S(1)} %bitcast.10, f32[448,768]{1,0:T(8,128)S(1)} %bitcast.8), custom_call_target="tpu_custom_call" | custom-call | tf_op jit(solution)/shard_map/update/pallas_call | solution.py:541
Async XLA Ops:
  0.6 71.5 %copy-start = (f32[2,224,768]{2,1,0:T(8,128)S(1)}, f32[2,224,768]{2,1,0:T(8,128)}, u32[]{:S(2)}) copy-start(f32[2,224,768]{2,1,0:T(8,128)} %param.5) | copy-start | bytes 4128772
